TPU v7x, 256 devices: a whole 4x4x8 slice. The times are simulated.
256 devices in a mesh: lon: 32 (over x_hi, z, core), lat: 8 (over x_lo, y).
Axes of the slice: x: 4 (x_hi: 2, x_lo: 2; x = x_hi * 2 + x_lo), y: 4, z: 8, core: 2. Of those that a mesh axis runs over, the one named last changes fastest.
Arguments:
- earlier_state: float32 [4, 4, 512, 16384], P(None, None, 'lat', 'lon'), may hold values from -6 to 6
- present_state: float32 [4, 4, 512, 16384], P(None, None, 'lat', 'lon'), may hold values from -6 to 6
- scalar_wet_flags: int32 [4, 512, 16384], P(None, 'lat', 'lon'), may hold values 0 or 1
- eastside_wet_flags: int32 [4, 512, 16384], P(None, 'lat', 'lon'), may hold values 0 or 1
- northside_wet_flags: int32 [4, 512, 16384], P(None, 'lat', 'lon'), may hold values 0 or 1
Outputs:
- after: float32 [4, 4, 512, 16384], P(None, None, 'lat', 'lon')
- filtered: float32 [4, 4, 512, 16384], P(None, None, 'lat', 'lon')
All inputs are finite; a program needn't handle non-finite values. No bound on the sum of `scalar_wet_flags` or of `eastside_wet_flags` or of `northside_wet_flags` on one device may be relied on, other than what follows from the above.
Results may differ from a plain program's by a relative error of at most 0.00002.
Values sent between devices are 32-bit elements; how exact they have to be, the bound alone decides.
A program may use at most 128 MiB of HBM per device.

v0:
```python
import jax
import jax.numpy as jnp
from jax import lax
from jax.sharding import PartitionSpec as P

advect_coef = 0.5
diffuse_coef = 0.25
twice_step = 0.5
gravity = 0.5
coriolis = 0.5
thermal = 0.2
haline = 0.15
asselin = 0.1


def from_partner(x, axis, stride):
    return lax.ppermute(x, axis, [(i, i ^ 1 << stride) for i in range(lax.axis_size(axis))])


def passed_along(x, axis, by):
    length = lax.axis_size(axis)
    return lax.ppermute(x, axis, [(i, (i + by) % length) for i in range(length)])


def passed_along_2(x, axis, by):
    length = lax.axis_size(axis)
    pairs = [(i, i + by) for i in range(length) if 0 <= i + by < length]
    return lax.ppermute(x, axis, pairs)


def pressure(temp, salt):
    density = haline * salt - thermal * temp
    return jnp.cumsum(density, axis=0) - 0.5 * density


def face_flux(here, ahead, speed, face_mask):
    return advect_coef * speed * (here[:4] + ahead[:4]) * 0.5 - diffuse_coef * face_mask * (
        ahead[4:] - here[4:]
    )


def shards(earlier_state, present_state, scalar_wet_flags, eastside_wet_flags, northside_wet_flags):
    tracer_cell_mask = scalar_wet_flags.astype(jnp.float32)
    mask_u = eastside_wet_flags.astype(jnp.float32)
    southnorth_wet_flags = northside_wet_flags.astype(jnp.float32)
    fmask = jnp.stack([tracer_cell_mask, tracer_cell_mask, mask_u, southnorth_wet_flags])
    curm = present_state * fmask
    befm = earlier_state * fmask
    both = jnp.concatenate([curm, befm], 0)
    height = both.shape[2]
    signs = jnp.array([1.0, 1.0, -1.0, -1.0, 1.0, 1.0, -1.0, -1.0], jnp.float32)[:, None, None]
    top_rows = both[:, :, -1, :]
    mirror = top_rows
    for bit in range(lax.axis_size("lon").bit_length() - 1):
        mirror = from_partner(mirror, "lon", bit)
    mirror = mirror[..., ::-1]
    ghost = mirror * signs
    is_top = lax.axis_index("lat") == lax.axis_size("lat") - 1
    east_col = passed_along(both[:, :, :, :1], "lon", -1)
    east = jnp.concatenate([both[:, :, :, 1:], east_col], 3)
    above_row = passed_along_2(both[:, :, :1, :], "lat", -1)
    north_row = jnp.where(is_top, ghost, above_row[:, :, 0, :])
    north = jnp.concatenate([both[:, :, 1:, :], north_row[:, :, None, :]], 2)
    flux_e = face_flux(both, east, curm[2], mask_u)
    northern_face_flux = face_flux(both, north, curm[3], southnorth_wet_flags)
    west_col = passed_along(flux_e[:, :, :, -1:], "lon", 1)
    flux_w = jnp.concatenate([west_col, flux_e[:, :, :, :-1]], 3)
    south_row = passed_along_2(northern_face_flux[:, :, -1:, :], "lat", 1)
    flux_s = jnp.concatenate([south_row, northern_face_flux[:, :, :-1, :]], 2)
    pres = pressure(curm[0], curm[1])
    pres_e = pressure(east[0], east[1])
    pres_n = pressure(north[0], north[1])
    global_rows = (lax.axis_index("lat") * height + jnp.arange(height, dtype=jnp.int32)).astype(
        jnp.float32
    )
    total_rows = height * lax.axis_size("lat")
    cor = (coriolis * (2.0 * (global_rows + 0.5) / total_rows - 1.0))[:, None]
    tend = -(flux_e - flux_w + (northern_face_flux - flux_s))
    zonal_velocity_tendency = tend[2] + (cor * curm[3] - gravity * mask_u * (pres_e - pres))
    tend_v = tend[3] - (cor * curm[2] + gravity * southnorth_wet_flags * (pres_n - pres))
    tend = jnp.stack([tend[0], tend[1], zonal_velocity_tendency, tend_v])
    after = (befm + twice_step * tend) * fmask
    filtered = curm + asselin * (befm - 2.0 * curm + after)
    return (after, filtered)


def solution(mesh):
    placed = (
        P(None, None, "lat", "lon"),
        P(None, None, "lat", "lon"),
        P(None, "lat", "lon"),
        P(None, "lat", "lon"),
        P(None, "lat", "lon"),
    )
    return jax.shard_map(
        shards,
        mesh=mesh,
        in_specs=placed,
        out_specs=(P(None, None, "lat", "lon"), P(None, None, "lat", "lon")),
        check_vma=False,
    )
```

profile of v0, /device:TPU:24, one launch (start us, length us, event | category | flops | bytes accessed | tf_op | source)
XLA Modules:
  0.0 92.9 jit_solution(4044842434828333324)
XLA Ops:
  0.6 1.2 %convert_bitcast_fusion.2 = f32[1,4,64,512]{3,2,1,0:T(8,128)S(1)} fusion(s32[4,64,512]{2,1,0:T(8,128)} %param.8), kind=kLoop, calls=%fused_computation.80 | loop fusion | flops 131072 | bytes 1048576 | tf_op jit(solution)/shard_map/stack | solution.py:46
  1.9 1.5 %convert_bitcast_fusion = (f32[1,4,64,512]{3,2,1,0:T(8,128)S(1)}, f32[1,4,64,512]{3,2,1,0:T(8,128)S(1)}) fusion(s32[4,64,512]{2,1,0:T(8,128)} %param.10, s32[4,64,512]{2,1,0:T(8,128)} %param.9), kind=kLoop, calls=%fused_computation.77 | loop fusion | flops 262144 | bytes 2097152 | tf_op jit(solution)/shard_map/stack | solution.py:46
  3.4 2.7 %fusion.27 = (f32[4,4,64,512]{3,2,1,0:T(8,128)S(1)}, f32[4,4,64,512]{3,2,1,0:T(8,128)S(1)}) fusion(f32[4,4,64,512]{3,2,1,0:T(8,128)S(1)} %copy-done.16, f32[1,4,64,512]{3,2,1,0:T(8,128)S(1)} %get-tuple-element.18, f32[1,4,64,512]{3,2,1,0:T(8,128)S(1)} %get-tuple-element.19, f32[1,4,64,512]{3,2,1,0:T(8,128)S(1)} %convert_bitcast_fusion.2, ...), kind=kLoop, calls=%fused_computation.49 | loop fusion | flops 2621440 | bytes 9961472 | tf_op jit(solution)/shard_map/mul | solution.py:48
  6.1 1.4 %copy_dynamic-update-slice_fusion.1 = f32[8,4,64,512]{3,1,0,2:T(4,128)S(1)} fusion(f32[4,4,64,512]{3,2,1,0:T(8,128)S(1)} %get-tuple-element.17), kind=kLoop, calls=%fused_computation.37 | loop fusion | bytes 4194304
  7.5 1.5 %copy_dynamic-update-slice_fusion = f32[8,4,64,512]{3,1,0,2:T(4,128)S(1)} fusion(f32[8,4,64,512]{3,1,0,2:T(4,128)S(1)} %copy_dynamic-update-slice_fusion.1, f32[4,4,64,512]{3,2,1,0:T(8,128)S(1)} %get-tuple-element.16), kind=kLoop, calls=%fused_computation.36 | loop fusion | bytes 4194304 | tf_op jit(solution)/shard_map/concatenate | solution.py:49
  9.1 2.9 %collective-permute-start.7 = (f32[8,4,1,512]{3,1,0,2:T(4,128)S(1)}, f32[8,4,1,512]{3,1,0,2:T(4,128)S(1)}, u32[]{:S(2)}, u32[]{:S(2)}) collective-permute-start(f32[8,4,1,512]{3,1,0,2:T(4,128)S(1)} %get-tuple-element.11), channel_id=1, source_target_pairs={{1,0},{2,1},{3,2},{4,3},{5,4},{6,5},{7,6},{9,8},{10,9},{11,10},{12... | collective-permute-start | bytes 196616 | tf_op jit(solution)/shard_map/ppermute | solution.py:28
  12.1 1.2 %slice.102 = f32[8,4,64,1]{3,1,0,2:T(4,128)} slice(f32[8,4,64,512]{3,1,0,2:T(4,128)S(1)} %copy_dynamic-update-slice_fusion), slice={[0:8], [0:4], [0:64], [0:1]} | slice | bytes 16384 | tf_op jit(solution)/shard_map/slice | solution.py:59
  13.3 1.8 %copy.47 = f32[8,4,64,1]{2,0,3,1:T(8,128)S(1)} copy(f32[8,4,64,1]{3,1,0,2:T(4,128)} %slice.102) | data formatting | bytes 16384 | tf_op jit(solution)/shard_map/slice | solution.py:59
  15.0 8.0 %collective-permute-start = (f32[8,4,64,1]{2,0,3,1:T(8,128)S(1)}, f32[8,4,64,1]{2,0,3,1:T(8,128)S(1)}, u32[]{:S(2)}, u32[]{:S(2)}) collective-permute-start(f32[8,4,64,1]{2,0,3,1:T(8,128)S(1)} %copy.47), channel_id=1, source_target_pairs={{0,248},{8,0},{16,8},{24,16},{32,24},{40,32},{48,40},{56,48},{64,5... | collective-permute-start | bytes 24584 | tf_op jit(solution)/shard_map/ppermute | solution.py:22
  24.1 1.1 %multiply_bitcast_fusion = (f32[4,64,512]{2,1,0:T(8,128)}, f32[4,64,512]{2,1,0:T(8,128)}) fusion(f32[4,4,64,512]{3,2,1,0:T(8,128)S(1)} %get-tuple-element.17), kind=kLoop, calls=%fused_computation.74 | loop fusion | flops 262144 | bytes 2097152 | tf_op jit(solution)/shard_map/mul | solution.py:37
  25.3 3.1 %collective-permute-done.3 = f32[8,4,512]{2,1,0:T(4,128)S(1)} collective-permute-done((f32[8,4,512]{2,1,0:T(4,128)S(1)}, f32[8,4,512]{2,1,0:T(4,128)S(1)}, u32[]{:S(2)}, u32[]{:S(2)}) %collective-permute-start.3) | collective-permute-done | bytes 65568 | tf_op jit(solution)/shard_map/ppermute | solution.py:17
  29.3 5.8 %collective-permute-done.4 = f32[8,4,512]{2,1,0:T(4,128)S(1)} collective-permute-done((f32[8,4,512]{2,1,0:T(4,128)S(1)}, f32[8,4,512]{2,1,0:T(4,128)S(1)}, u32[]{:S(2)}, u32[]{:S(2)}) %collective-permute-start.4) | collective-permute-done | bytes 65568 | tf_op jit(solution)/shard_map/ppermute | solution.py:17
  35.1 5.6 %slice.110 = f32[8,4,63,512]{3,1,0,2:T(4,128)} slice(f32[8,4,64,512]{3,1,0,2:T(4,128)} %copy-done.3), slice={[0:8], [0:4], [1:64], [0:512]} | slice | bytes 8257536 | tf_op jit(solution)/shard_map/slice | solution.py:63
  40.7 4.2 %slice.101 = f32[8,4,64,511]{3,1,0,2:T(4,128)} slice(f32[8,4,64,512]{3,1,0,2:T(4,128)S(1)} %copy-done.4), slice={[0:8], [0:4], [0:64], [1:512]} | slice | bytes 8372224 | tf_op jit(solution)/shard_map/slice | solution.py:60
  44.9 6.7 %copy.48 = f32[8,4,64,511]{3,2,1,0:T(8,128)} copy(f32[8,4,64,511]{3,1,0,2:T(4,128)} %slice.101) | data formatting | bytes 8372224 | tf_op jit(solution)/shard_map/slice | solution.py:60
  51.7 4.4 %copy.52 = f32[8,4,63,512]{3,2,1,0:T(8,128)} copy(f32[8,4,63,512]{3,1,0,2:T(4,128)S(1)} %copy-done.5) | data formatting | bytes 8257536 | tf_op jit(solution)/shard_map/slice | solution.py:63
  57.5 3.1 %fusion.24 = f32[4,64,512]{2,1,0:T(8,128)} fusion(f32[4,64,512]{2,1,0:T(8,128)} %reduce-window_subtract_fusion.1, f32[8,4,64,1]{3,2,1,0:T(8,128)S(1)} %copy.49, f32[8,4,64,511]{3,2,1,0:T(8,128)} %copy.48, s32[4,64,512]{2,1,0:T(8,128)} %param.9, f32[4,4,64,512]{3,2,1,0:T(8,128)S(1)} %get-tuple-element.17, f32[64]{0:T(128)S(1)} %add_multiply_fusion), kind=kOutput, calls=%fused_computation.46 | output fusion | flops 2752512 | bytes 12583424 | tf_op jit(solution)/shard_map/jit(cumsum)/reduce_window_sum | solution.py:33
  60.6 1.8 %collective-permute-done.6 = f32[8,4,512]{2,1,0:T(4,128)S(1)} collective-permute-done((f32[8,4,512]{2,1,0:T(4,128)S(1)}, f32[8,4,512]{2,1,0:T(4,128)S(1)}, u32[]{:S(2)}, u32[]{:S(2)}) %collective-permute-start.6) | collective-permute-done | bytes 65568 | tf_op jit(solution)/shard_map/ppermute | solution.py:17
  63.0 5.8 %fusion.4 = (f32[4,4,64,512]{3,2,1,0:T(8,128)S(1)}, f32[4,4,64,512]{3,2,1,0:T(8,128)S(1)}) fusion(f32[4,4,64,512]{3,2,1,0:T(8,128)S(1)} %get-tuple-element.17, f32[8,4,63,512]{3,2,1,0:T(8,128)} %copy.52, f32[4,4,64,512]{3,2,1,0:T(8,128)} %copy-done.1, f32[8,4,1,512]{3,2,1,0:T(1,128)S(1)} %broadcast_in_dim.2, f32[4,64,512]{2,1,0:T(8,128)} %get-tuple-element.20, ...), kind=kLoop, calls=%fused_computation.16 | loop fusion | flops 8388608 | bytes 18874368 | tf_op jit(solution)/shard_map/sub | solution.py:37
  68.9 4.1 %collective-permute-start.8 = (f32[4,4,1,512]{3,2,1,0:T(1,128)S(1)}, f32[4,4,1,512]{3,2,1,0:T(1,128)S(1)}, u32[]{:S(2)}, u32[]{:S(2)}) collective-permute-start(f32[4,4,1,512]{3,2,1,0:T(1,128)S(1)} %slice.117), channel_id=1, source_target_pairs={{0,1},{1,2},{2,3},{3,4},{4,5},{5,6},{6,7},{8,9},{9,10},{10,11},{11... | collective-permute-start | bytes 98312 | tf_op jit(solution)/shard_map/ppermute | solution.py:28
  73.8 11.9 %collective-permute-done.1 = f32[4,4,64,1]{3,2,1,0:T(8,128)S(1)} collective-permute-done((f32[4,4,64,1]{3,2,1,0:T(8,128)S(1)}, f32[4,4,64,1]{3,2,1,0:T(8,128)S(1)}, u32[]{:S(2)}, u32[]{:S(2)}) %collective-permute-start.1) | collective-permute-done | bytes 4128 | tf_op jit(solution)/shard_map/ppermute | solution.py:22
  85.7 1.3 %fusion.17 = f32[4,4,64,512]{3,2,1,0:T(8,128)S(1)} fusion(f32[4,4,64,512]{3,2,1,0:T(8,128)S(1)} %get-tuple-element.9, f32[4,4,64,511]{3,2,1,0:T(8,128)S(1)} %bitcast.58, f32[4,4,64,1]{3,2,1,0:T(8,128)S(1)} %collective-permute-done.1, f32[4,4,64,512]{3,2,1,0:T(8,128)S(1)} %get-tuple-element.8, f32[4,4,63,512]{3,2,1,0:T(8,128)S(1)} %bitcast.59, ...), kind=kLoop, calls=%fused_computation.31 | loop fusion | flops 3145728 | bytes 10485760 | tf_op jit(solution)/shard_map/neg | solution.py:78
  88.2 1.4 %copy-done.2 = f32[4,4,64,512]{3,2,1,0:T(8,128)S(1)} copy-done((f32[4,4,64,512]{3,2,1,0:T(8,128)S(1)}, f32[4,4,64,512]{3,2,1,0:T(8,128)}, u32[]{:S(2)}) %copy-start.2) | copy-done | bytes 2097176
  89.9 3.0 %multiply_add_fusion = (f32[4,4,64,512]{3,2,1,0:T(8,128)}, f32[4,4,64,512]{3,2,1,0:T(8,128)}) fusion(f32[4,4,64,512]{3,2,1,0:T(8,128)S(1)} %get-tuple-element.17, f32[4,4,64,512]{3,2,1,0:T(8,128)S(1)} %copy-done.2, f32[1,4,64,512]{3,2,1,0:T(8,128)S(1)} %copy-done.9, f32[1,4,64,512]{3,2,1,0:T(8,128)S(1)} %copy-done.11, f32[1,4,64,512]{3,2,1,0:T(8,128)S(1)} %copy-done.7, ...), kind=kLoop, calls=%fused_computation.38 | loop fusion | flops 6815744 | bytes 12058624 | tf_op jit(solution)/shard_map/add | solution.py:83
  (61 shorter events, 6.4 us)
Async XLA Ops:
  0.6 2.8 %copy-start.16 = (f32[4,4,64,512]{3,2,1,0:T(8,128)S(1)}, f32[4,4,64,512]{3,2,1,0:T(8,128)}, u32[]{:S(2)}) copy-start(f32[4,4,64,512]{3,2,1,0:T(8,128)} %param.6) | copy-start | bytes 6291460
  1.9 4.2 %copy-start.6 = (f32[1,4,64,512]{3,2,1,0:T(8,128)}, f32[1,4,64,512]{3,2,1,0:T(8,128)S(1)}, u32[]{:S(2)}) copy-start(f32[1,4,64,512]{3,2,1,0:T(8,128)S(1)} %convert_bitcast_fusion.2) | copy-start | bytes 1572868
  3.4 2.7 %copy-start.8 = (f32[1,4,64,512]{3,2,1,0:T(8,128)}, f32[1,4,64,512]{3,2,1,0:T(8,128)S(1)}, u32[]{:S(2)}) copy-start(f32[1,4,64,512]{3,2,1,0:T(8,128)S(1)} %get-tuple-element.18) | copy-start | bytes 1572868
  3.4 2.7 %copy-start.10 = (f32[1,4,64,512]{3,2,1,0:T(8,128)}, f32[1,4,64,512]{3,2,1,0:T(8,128)S(1)}, u32[]{:S(2)}) copy-start(f32[1,4,64,512]{3,2,1,0:T(8,128)S(1)} %get-tuple-element.19) | copy-start | bytes 1572868
  9.0 3.1 %copy-start.3 = (f32[8,4,64,512]{3,1,0,2:T(4,128)}, f32[8,4,64,512]{3,1,0,2:T(4,128)S(1)}, u32[]{:S(2)}) copy-start(f32[8,4,64,512]{3,1,0,2:T(4,128)S(1)} %copy_dynamic-update-slice_fusion) | copy-start | bytes 12582916
  9.0 14.1 %copy-start.12 = (s32[4,64,512]{2,1,0:T(8,128)S(1)}, s32[4,64,512]{2,1,0:T(8,128)}, u32[]{:S(2)}) copy-start(s32[4,64,512]{2,1,0:T(8,128)} %param.9) | copy-start | bytes 1572868
  9.0 14.1 %copy-start.14 = (s32[4,64,512]{2,1,0:T(8,128)S(1)}, s32[4,64,512]{2,1,0:T(8,128)}, u32[]{:S(2)}) copy-start(s32[4,64,512]{2,1,0:T(8,128)} %param.10) | copy-start | bytes 1572868
  9.0 15.1 %collective-permute-start.2 = (f32[8,4,512]{2,1,0:T(4,128)S(1)}, f32[8,4,512]{2,1,0:T(4,128)S(1)}, u32[]{:S(2)}, u32[]{:S(2)}) collective-permute-start(f32[8,4,512]{2,1,0:T(4,128)S(1)} %get-tuple-element.10), channel_id=1, source_target_pairs={{0,8},{8,0},{16,24},{24,16},{32,40},{40,32},{48,56},{56,48},{64,72... | collective-permute-start | bytes 196616 | tf_op jit(solution)/shard_map/ppermute | solution.py:17
  9.1 53.7 %collective-permute-start.7 = (f32[8,4,1,512]{3,1,0,2:T(4,128)S(1)}, f32[8,4,1,512]{3,1,0,2:T(4,128)S(1)}, u32[]{:S(2)}, u32[]{:S(2)}) collective-permute-start(f32[8,4,1,512]{3,1,0,2:T(4,128)S(1)} %get-tuple-element.11), channel_id=1, source_target_pairs={{1,0},{2,1},{3,2},{4,3},{5,4},{6,5},{7,6},{9,8},{10,9},{11,10},{12... | collective-permute-start | bytes 196616 | tf_op jit(solution)/shard_map/ppermute | solution.py:28
  15.0 41.1 %collective-permute-start = (f32[8,4,64,1]{2,0,3,1:T(8,128)S(1)}, f32[8,4,64,1]{2,0,3,1:T(8,128)S(1)}, u32[]{:S(2)}, u32[]{:S(2)}) collective-permute-start(f32[8,4,64,1]{2,0,3,1:T(8,128)S(1)} %copy.47), channel_id=1, source_target_pairs={{0,248},{8,0},{16,8},{24,16},{32,24},{40,32},{48,40},{56,48},{64,5... | collective-permute-start | bytes 24584 | tf_op jit(solution)/shard_map/ppermute | solution.py:22
  24.1 4.3 %collective-permute-start.3 = (f32[8,4,512]{2,1,0:T(4,128)S(1)}, f32[8,4,512]{2,1,0:T(4,128)S(1)}, u32[]{:S(2)}, u32[]{:S(2)}) collective-permute-start(f32[8,4,512]{2,1,0:T(4,128)S(1)} %collective-permute-done.2), channel_id=1, source_target_pairs={{0,16},{8,24},{16,0},{24,8},{32,48},{40,56},{48,32},{56,40},{64,80... | collective-permute-start | bytes 196616 | tf_op jit(solution)/shard_map/ppermute | solution.py:17
  28.4 6.7 %collective-permute-start.4 = (f32[8,4,512]{2,1,0:T(4,128)S(1)}, f32[8,4,512]{2,1,0:T(4,128)S(1)}, u32[]{:S(2)}, u32[]{:S(2)}) collective-permute-start(f32[8,4,512]{2,1,0:T(4,128)S(1)} %collective-permute-done.3), channel_id=1, source_target_pairs={{0,32},{8,40},{16,48},{24,56},{32,0},{40,8},{48,16},{56,24},{64,96... | collective-permute-start | bytes 196616 | tf_op jit(solution)/shard_map/ppermute | solution.py:17
  35.1 21.4 %collective-permute-start.5 = (f32[8,4,512]{2,1,0:T(4,128)S(1)}, f32[8,4,512]{2,1,0:T(4,128)S(1)}, u32[]{:S(2)}, u32[]{:S(2)}) collective-permute-start(f32[8,4,512]{2,1,0:T(4,128)S(1)} %collective-permute-done.4), channel_id=1, source_target_pairs={{0,64},{8,72},{16,80},{24,88},{32,96},{40,104},{48,112},{56,120},{... | collective-permute-start | bytes 196616 | tf_op jit(solution)/shard_map/ppermute | solution.py:17
  35.1 5.6 %copy-start.4 = (f32[8,4,64,512]{3,1,0,2:T(4,128)S(1)}, f32[8,4,64,512]{3,1,0,2:T(4,128)}, u32[]{:S(2)}) copy-start(f32[8,4,64,512]{3,1,0,2:T(4,128)} %copy-done.3) | copy-start | bytes 12582916
  44.9 6.7 %copy-start.5 = (f32[8,4,63,512]{3,1,0,2:T(4,128)S(1)}, f32[8,4,63,512]{3,1,0,2:T(4,128)}, u32[]{:S(2)}) copy-start(f32[8,4,63,512]{3,1,0,2:T(4,128)} %slice.110) | copy-start | bytes 12386308
  56.5 6.3 %copy-start.18 = (f32[8]{0:T(128)S(1)}, f32[8]{0:T(128)}, u32[]{:S(2)}) copy-start(f32[8]{0:T(128)} %constant.38.clone) | copy-start | bytes 100
  56.5 5.9 %collective-permute-start.6 = (f32[8,4,512]{2,1,0:T(4,128)S(1)}, f32[8,4,512]{2,1,0:T(4,128)S(1)}, u32[]{:S(2)}, u32[]{:S(2)}) collective-permute-start(f32[8,4,512]{2,1,0:T(4,128)S(1)} %collective-permute-done.5), channel_id=1, source_target_pairs={{0,128},{8,136},{16,144},{24,152},{32,160},{40,168},{48,176},{56,1... | collective-permute-start | bytes 196616 | tf_op jit(solution)/shard_map/ppermute | solution.py:17
  63.0 10.5 %copy-start = (f32[8,4,63,512]{3,2,1,0:T(8,128)S(1)}, f32[8,4,63,512]{3,2,1,0:T(8,128)}, u32[]{:S(2)}) copy-start(f32[8,4,63,512]{3,2,1,0:T(8,128)} %copy.52) | copy-start | bytes 12386308
  63.0 10.5 %copy-start.13 = (f32[4,64,512]{2,1,0:T(8,128)S(1)}, f32[4,64,512]{2,1,0:T(8,128)}, u32[]{:S(2)}) copy-start(f32[4,64,512]{2,1,0:T(8,128)} %reduce-window_subtract_fusion.1) | copy-start | bytes 1572868
  63.0 10.5 %copy-start.15 = (s32[4,64,512]{2,1,0:T(8,128)S(1)}, s32[4,64,512]{2,1,0:T(8,128)}, u32[]{:S(2)}) copy-start(s32[4,64,512]{2,1,0:T(8,128)} %param.10) | copy-start | bytes 1572868
  68.9 16.8 %collective-permute-start.8 = (f32[4,4,1,512]{3,2,1,0:T(1,128)S(1)}, f32[4,4,1,512]{3,2,1,0:T(1,128)S(1)}, u32[]{:S(2)}, u32[]{:S(2)}) collective-permute-start(f32[4,4,1,512]{3,2,1,0:T(1,128)S(1)} %slice.117), channel_id=1, source_target_pairs={{0,1},{1,2},{2,3},{3,4},{4,5},{5,6},{6,7},{8,9},{9,10},{10,11},{11... | collective-permute-start | bytes 98312 | tf_op jit(solution)/shard_map/ppermute | solution.py:28
  73.2 12.5 %collective-permute-start.1 = (f32[4,4,64,1]{3,2,1,0:T(8,128)S(1)}, f32[4,4,64,1]{3,2,1,0:T(8,128)S(1)}, u32[]{:S(2)}, u32[]{:S(2)}) collective-permute-start(f32[4,4,64,1]{3,2,1,0:T(8,128)S(1)} %slice.107), channel_id=1, source_target_pairs={{0,8},{8,16},{16,24},{24,32},{32,40},{40,48},{48,56},{56,64},{64,7... | collective-permute-start | bytes 12296 | tf_op jit(solution)/shard_map/ppermute | solution.py:22
  88.0 1.7 %copy-start.7 = (f32[1,4,64,512]{3,2,1,0:T(8,128)S(1)}, f32[1,4,64,512]{3,2,1,0:T(8,128)}, u32[]{:S(2)}) copy-start(f32[1,4,64,512]{3,2,1,0:T(8,128)} %copy-done.6) | copy-start | bytes 1572868
  88.0 1.9 %copy-start.9 = (f32[1,4,64,512]{3,2,1,0:T(8,128)S(1)}, f32[1,4,64,512]{3,2,1,0:T(8,128)}, u32[]{:S(2)}) copy-start(f32[1,4,64,512]{3,2,1,0:T(8,128)} %copy-done.8) | copy-start | bytes 1572868
  (4 other events, 5.3 us)
where the time goes:
time: 93.2 us; the launch traced here: 92.9 us
  local copies, waits for them, and re-layouts  30.6 us (33%)
  waiting for transfers between devices  22.7 us (24%)
  other arithmetic  22.2 us (24%)
  starting transfers between devices  16.4 us (18%)
  between operations  1.01 us (1%)
    ppermute x2, waiting for transfers between devices, passed_along(): lax.ppermute(x, axis, [(i, (i + by) % length) for i in range(length)])  11.9 us
    slice x2, local copies, waits for them, and re-layouts, shards(): east = jnp.concatenate([both[:, :, :, 1:], east_col], 3)  11 us
    ppermute x5, waiting for transfers between devices, from_partner(): lax.ppermute(x, axis, [(i, i ^ 1 << stride) for i in range(lax.axis_size(...  10.7 us
    slice x2, local copies, waits for them, and re-layouts, shards(): north = jnp.concatenate([both[:, :, 1:, :], north_row[:, :, None, :]], 2)  9.97 us
    ppermute x2, starting transfers between devices, passed_along(): lax.ppermute(x, axis, [(i, (i + by) % length) for i in range(length)])  8.33 us
    ppermute x2, starting transfers between devices, passed_along_2(): return lax.ppermute(x, axis, pairs)  7 us
    sub x1, other arithmetic, face_flux(): advect_coef * speed * (here[:4] + ahead[:4]) * 0.5  5.84 us
    another operation x3, other arithmetic, pressure(): return jnp.cumsum(density, axis=0) - 0.5 * density  4.21 us
  transfers between devices with their start and end apart: 9, of which 4 were waited for; matrix products, arithmetic and copies ran while one was open for 34% of the time, Pallas kernels for 0%

commit v1 on v0

v1 whole, which is shorter than its diff:
```python
import functools

import jax
import jax.numpy as jnp
from jax import lax
from jax.experimental import pallas as pl
from jax.experimental.pallas import tpu as pltpu
from jax.sharding import PartitionSpec as P

advect_coef = 0.5
diffuse_coef = 0.25
twice_step = 0.5
gravity = 0.5
coriolis = 0.5
thermal = 0.2
haline = 0.15
asselin = 0.1

LANES = 128
SUB = 8
MESH = pl.DeviceIdType.MESH


def kernel(
    n_lon,
    n_lat,
    bef_hbm,
    cur_hbm,
    tm_hbm,
    um_hbm,
    vm_hbm,
    after_ref,
    filt_ref,
    st,
    mk,
    pr,
    fn,
    send_w,
    send_e,
    from_e,
    from_w,
    pres_e,
    fold,
    load_sems,
    send_sems,
    recv_sems,
):
    levels, rows, cols = tm_hbm.shape
    chunks = cols // LANES
    strips = rows // SUB
    lon, lat = lax.axis_index("lon"), lax.axis_index("lat")
    east, west = lax.rem(lon + 1, n_lon), lax.rem(lon + n_lon - 1, n_lon)
    partner = n_lon - 1 - lon
    has_north, has_south = lat < n_lat - 1, lat > 0
    is_top = lat == n_lat - 1

    barrier = pltpu.get_barrier_semaphore()
    pl.semaphore_signal(barrier, inc=1, device_id={"lon": east}, device_id_type=MESH)
    pl.semaphore_signal(barrier, inc=1, device_id={"lon": west}, device_id_type=MESH)

    @pl.when(has_north)
    def _():
        pl.semaphore_signal(barrier, inc=1, device_id={"lat": lat + 1}, device_id_type=MESH)

    @pl.when(has_south)
    def _():
        pl.semaphore_signal(barrier, inc=1, device_id={"lat": lat - 1}, device_id_type=MESH)

    @pl.when(is_top)
    def _():
        pl.semaphore_signal(barrier, inc=1, device_id={"lon": partner}, device_id_type=MESH)

    loads = []
    for i, t in enumerate(range(chunks)):
        lanes = pl.ds(LANES * t, LANES)
        inside = pl.ds(SUB, rows)
        for j, (src, dst) in enumerate(
            [
                (cur_hbm.at[:, :, :, lanes], st.at[t, 0:4, :, inside, :]),
                (bef_hbm.at[:, :, :, lanes], st.at[t, 4:8, :, inside, :]),
                (tm_hbm.at[:, :, lanes], mk.at[t, 0]),
                (um_hbm.at[:, :, lanes], mk.at[t, 1]),
                (vm_hbm.at[:, :, lanes], mk.at[t, 2]),
            ]
        ):
            copy = pltpu.make_async_copy(src, dst, load_sems.at[t, j])
            copy.start()
            loads.append(copy)
    for copy in loads:
        copy.wait()

    lane = lax.broadcasted_iota(jnp.int32, (SUB, LANES), 1)

    def mask_strip(r, carry):
        strip = pl.ds(pl.multiple_of(SUB + SUB * r, SUB), SUB)
        plain = pl.ds(pl.multiple_of(SUB * r, SUB), SUB)
        pack_w = jnp.zeros((SUB, LANES), jnp.float32)
        pack_e = jnp.zeros((SUB, LANES), jnp.float32)
        for t in range(chunks):
            total = None
            for l in range(levels):
                m = [mk[t, i, l, plain, :].astype(jnp.float32) for i in range(3)]
                fm = [m[0], m[0], m[1], m[2]]
                x = [None] * 8
                for f in range(8):
                    x[f] = st[t, f, l, strip, :] * fm[f % 4]
                    st[t, f, l, strip, :] = x[f]
                    c = f * levels + l
                    if t == 0:
                        moved = x[f] if c == 0 else pltpu.roll(x[f], c, 1)
                        pack_w = jnp.where(lane == c, moved, pack_w)
                    if t == chunks - 1:
                        pack_e = jnp.where(lane == c, pltpu.roll(x[f], c + 1, 1), pack_e)
                if t == chunks - 1:
                    c = 8 * levels + l
                    pack_e = jnp.where(lane == c, pltpu.roll(m[1], c + 1, 1), pack_e)
                rho = haline * x[1] - thermal * x[0]
                total = rho if total is None else total + rho
                pr[t, l, strip, :] = total - 0.5 * rho
                st[t, 8, l, strip, :] = m[2]
        send_w[plain, :] = pack_w
        send_e[plain, :] = pack_e
        return carry

    lax.fori_loop(0, strips, mask_strip, 0)

    @pl.when(has_south)
    def _():
        pl.semaphore_wait(barrier, 4)

    @pl.when(lat == 0)
    def _():
        pl.semaphore_wait(barrier, 3)

    def remote(src, dst, which, device):
        return pltpu.make_async_remote_copy(
            src_ref=src,
            dst_ref=dst,
            send_sem=send_sems.at[which],
            recv_sem=recv_sems.at[which],
            device_id=device,
            device_id_type=MESH,
        )

    to_west = remote(send_w, from_e, 0, {"lon": west})
    to_east = remote(send_e, from_w, 1, {"lon": east})
    to_north = remote(
        st.at[:, :, :, pl.ds(rows + SUB - 1, 1), :],
        st.at[:, :, :, pl.ds(SUB - 1, 1), :],
        2,
        {"lat": lat + 1},
    )
    to_south = remote(
        st.at[:, 0:8, :, pl.ds(SUB, 1), :],
        st.at[:, 0:8, :, pl.ds(rows + SUB, 1), :],
        3,
        {"lat": lat - 1},
    )
    to_fold = remote(st.at[:, 0:8, :, rows + SUB - 1, :], fold, 4, {"lon": partner})

    @pl.when(is_top)
    def _():
        to_fold.start()

    to_west.start()
    to_east.start()

    @pl.when(has_north)
    def _():
        to_north.start()

    @pl.when(has_south)
    def _():
        to_south.start()

    @pl.when(lat == 0)
    def _():
        for t in range(chunks):
            for f in range(9):
                for l in range(levels):
                    st[t, f, l, 0:SUB, :] = jnp.zeros((SUB, LANES), jnp.float32)

    @pl.when(has_south)
    def _():
        to_north.wait_recv()

    @pl.when(has_north)
    def _():
        to_south.wait_recv()

    @pl.when(is_top)
    def _():
        to_fold.wait_recv()
        back = LANES - 1 - lax.broadcasted_iota(jnp.int32, (levels, LANES), 1)
        for t in range(chunks):
            for f in range(8):
                y = jnp.take_along_axis(
                    fold[chunks - 1 - t, f], back, axis=1, mode="promise_in_bounds"
                )
                if f % 4 >= 2:
                    y = -y
                for l in range(levels):
                    st[t, f, l, rows + SUB : rows + SUB + 1, :] = y[l : l + 1, :]

    to_west.wait_recv()
    to_east.wait_recv()

    def face(scaled_speed, scaled_mask, h, a):
        return [
            scaled_speed * (h[k] + a[k]) - scaled_mask * (a[4 + k] - h[4 + k]) for k in range(4)
        ]

    advect = advect_coef * 0.5 * twice_step
    diffuse = diffuse_coef * twice_step

    for t in range(chunks):
        total = None
        for l in range(levels):
            h = [st[t, f, l, 0:SUB, :] for f in range(8)]
            a = [st[t, f, l, 1 : SUB + 1, :] for f in range(8)]
            flux = face(advect * h[3], diffuse * st[t, 8, l, 0:SUB, :], h, a)
            for k in range(4):
                fn[t, k, l, 0:SUB, :] = flux[k]
            edge = slice(rows + SUB, rows + 2 * SUB)
            rho = haline * st[t, 1, l, edge, :] - thermal * st[t, 0, l, edge, :]
            total = rho if total is None else total + rho
            pr[t, l, edge, :] = total - 0.5 * rho

    def east_pressure(r, carry):
        plain = pl.ds(pl.multiple_of(SUB * r, SUB), SUB)
        x = from_e[plain, :]
        rho = haline * pltpu.roll(x, LANES - levels, 1) - thermal * x
        total = rho
        for l in range(1, levels):
            total = total + jnp.where(lane >= l, pltpu.roll(rho, l, 1), 0.0)
        pres_e[plain, :] = total - 0.5 * rho
        return carry

    lax.fori_loop(0, strips, east_pressure, 0)

    def step_strip(r, carry):
        at = pl.multiple_of(SUB + SUB * r, SUB)
        plain = pl.ds(pl.multiple_of(SUB * r, SUB), SUB)
        strip, above, below = pl.ds(at, SUB), pl.ds(at + 1, SUB), pl.ds(at - 1, SUB)
        row = lat * rows + r * SUB + lax.broadcasted_iota(jnp.int32, (SUB, LANES), 0)
        cor = coriolis * (2.0 * (row.astype(jnp.float32) + 0.5) / (rows * n_lat) - 1.0)
        cor = twice_step * cor
        edge_e, edge_w, edge_p = from_e[plain, :], from_w[plain, :], pres_e[plain, :]
        first, last = lane == 0, lane == LANES - 1

        def at_last(x, c):
            return pltpu.roll(x, LANES - 1 - c, 1)

        def at_first(x, c):
            return x if c == 0 else pltpu.roll(x, LANES - c, 1)

        for l in range(levels):
            h = [st[0, f, l, strip, :] for f in range(8)]
            p = pr[0, l, strip, :]
            back = [pltpu.roll(x, LANES - 1, 1) for x in h + [p]]
            w = [at_first(edge_w, f * levels + l) for f in range(8)]
            w_mask = at_first(edge_w, 8 * levels + l)
            prior = face(advect * w[2], diffuse * w_mask, w, h)
            for t in range(chunks):
                lanes = pl.ds(LANES * t, LANES)
                if t + 1 < chunks:
                    h_next = [st[t + 1, f, l, strip, :] for f in range(8)]
                    p_next = pr[t + 1, l, strip, :]
                    back_next = [pltpu.roll(x, LANES - 1, 1) for x in h_next + [p_next]]
                else:
                    h_next = p_next = None
                    back_next = [at_last(edge_e, f * levels + l) for f in range(8)]
                    back_next.append(at_last(edge_p, l))
                a = [jnp.where(last, y, x) for x, y in zip(back, back_next)]
                m = [mk[t, i, l, plain, :].astype(jnp.float32) for i in range(3)]
                fm = [m[0], m[0], m[1], m[2]]
                flux_e = face(advect * h[2], diffuse * m[1], h, a)
                moved = [pltpu.roll(x, 1, 1) for x in flux_e]
                flux_w = [jnp.where(first, y, x) for x, y in zip(moved, prior)]
                prior = moved
                n = [st[t, f, l, above, :] for f in range(8)]
                flux_n = face(advect * h[3], diffuse * m[2], h, n)
                for k in range(4):
                    fn[t, k, l, strip, :] = flux_n[k]
                tend = [
                    (flux_w[k] - flux_e[k]) + (fn[t, k, l, below, :] - flux_n[k]) for k in range(4)
                ]
                push = gravity * twice_step
                tend[2] = tend[2] + (cor * h[3] - push * m[1] * (a[8] - p))
                tend[3] = tend[3] - (cor * h[2] + push * m[2] * (pr[t, l, above, :] - p))
                for k in range(4):
                    after = (h[4 + k] + tend[k]) * fm[k]
                    after_ref[k, l, plain, lanes] = after
                    filt_ref[k, l, plain, lanes] = (1.0 - 2.0 * asselin) * h[k] + asselin * (
                        h[4 + k] + after
                    )
                h, p, back = h_next, p_next, back_next
        return carry

    lax.fori_loop(0, strips, step_strip, 0)

    to_west.wait_send()
    to_east.wait_send()

    @pl.when(has_north)
    def _():
        to_north.wait_send()

    @pl.when(has_south)
    def _():
        to_south.wait_send()

    @pl.when(is_top)
    def _():
        to_fold.wait_send()


def shards(n_lon, n_lat, *args):
    _, levels, rows, cols = args[0].shape
    chunks = cols // LANES
    f32 = jnp.float32
    out = jax.ShapeDtypeStruct(args[0].shape, f32)
    args = [pltpu.with_memory_space_constraint(x, pltpu.HBM) for x in args]
    return pl.pallas_call(
        functools.partial(kernel, n_lon, n_lat),
        out_shape=(out, out),
        in_specs=[pl.BlockSpec(memory_space=pl.ANY)] * 5,
        out_specs=(pl.BlockSpec(memory_space=pltpu.VMEM),) * 2,
        scratch_shapes=[
            pltpu.VMEM((chunks, 9, levels, rows + 2 * SUB, LANES), f32),
            pltpu.VMEM((chunks, 3, levels, rows, LANES), jnp.int32),
            pltpu.VMEM((chunks, levels, rows + 2 * SUB, LANES), f32),
            pltpu.VMEM((chunks, 4, levels, rows + 2 * SUB, LANES), f32),
            pltpu.VMEM((rows, LANES), f32),
            pltpu.VMEM((rows, LANES), f32),
            pltpu.VMEM((rows, LANES), f32),
            pltpu.VMEM((rows, LANES), f32),
            pltpu.VMEM((rows, LANES), f32),
            pltpu.VMEM((chunks, 8, levels, LANES), f32),
            pltpu.SemaphoreType.DMA((chunks, 5)),
            pltpu.SemaphoreType.DMA((5,)),
            pltpu.SemaphoreType.DMA((5,)),
        ],
        compiler_params=pltpu.CompilerParams(
            collective_id=0, has_side_effects=True, vmem_limit_bytes=28 << 20
        ),
    )(*args)


def solution(mesh):
    state = P(None, None, "lat", "lon")
    flags = P(None, "lat", "lon")
    return jax.shard_map(
        functools.partial(shards, mesh.shape["lon"], mesh.shape["lat"]),
        mesh=mesh,
        in_specs=(state, state, flags, flags, flags),
        out_specs=(state, state),
        check_vma=False,
    )
```

time: 93.2 us -> 28 us (0.30)
  the two profiles are of different devices: /device:TPU:24 before, /device:TPU:26 now
where the time goes in v1:
time: 28 us; the launch traced here: 27.5 us
  Pallas kernels  24.2 us (86%)
  local copies, waits for them, and re-layouts  2.64 us (9%)
  between operations  0.64 us (2%)
    pallas_call x1, Pallas kernels, shards(): pl.pallas_call(functools.partial(kernel, n_lon, n_lat), out_shape=(out, o...  24.2 us
    unnamed x2, local copies, waits for them, and re-layouts  2.64 us

profile of v1, /device:TPU:26, one launch (start us, length us, event | category | flops | bytes accessed | tf_op | source)
XLA Modules:
  0.0 27.5 jit_solution(5430334581028799412)
XLA Ops:
  0.6 24.2 %shard_map.68 = (f32[4,4,64,512]{3,2,1,0:T(8,128)S(1)}, f32[4,4,64,512]{3,2,1,0:T(8,128)S(1)}) custom-call(f32[4,4,64,512]{3,2,1,0:T(8,128)} %bef_hbm.1, f32[4,4,64,512]{3,2,1,0:T(8,128)} %cur_hbm.1, s32[4,64,512]{2,1,0:T(8,128)} %tm_hbm.1, s32[4,64,512]{2,1,0:T(8,128)} %um_hbm.1, s32[4,64,512]{2,1,0:T(8,128)} %vm_hbm.1), custom_call_target="tpu_custom_call" | custom-call | tf_op jit(solution)/shard_map/pallas_call | solution.py:324
  24.9 1.3 %copy.9 = f32[4,4,64,512]{3,2,1,0:T(8,128)} copy(f32[4,4,64,512]{3,2,1,0:T(8,128)S(1)} %get-tuple-element.4) | data formatting | bytes 4194304
  26.2 1.3 %copy.10 = f32[4,4,64,512]{3,2,1,0:T(8,128)} copy(f32[4,4,64,512]{3,2,1,0:T(8,128)S(1)} %get-tuple-element.5) | data formatting | bytes 4194304

commit v2 on v1

v2 whole, which is shorter than its diff:
```python
import functools

import jax
import jax.numpy as jnp
from jax import lax
from jax.experimental import pallas as pl
from jax.experimental.pallas import tpu as pltpu
from jax.sharding import PartitionSpec as P

advect_coef = 0.5
diffuse_coef = 0.25
twice_step = 0.5
gravity = 0.5
coriolis = 0.5
thermal = 0.2
haline = 0.15
asselin = 0.1

LANES = 128
SUB = 8
MESH = pl.DeviceIdType.MESH
DRY = 1e30


def kernel(
    n_lon,
    n_lat,
    bef_hbm,
    cur_hbm,
    tm_hbm,
    um_hbm,
    vm_hbm,
    after_ref,
    filt_ref,
    st,
    mk,
    pr,
    fn,
    own,
    from_e,
    from_w,
    top,
    bottom,
    from_n,
    from_s,
    load_sems,
    send_sems,
    recv_sems,
):
    levels, rows, cols = tm_hbm.shape
    chunks = cols // LANES
    strips = rows // SUB
    middle = range(1, chunks - 1)
    ends = sorted({0, chunks - 1})
    lon, lat = lax.axis_index("lon"), lax.axis_index("lat")
    east, west = lax.rem(lon + 1, n_lon), lax.rem(lon + n_lon - 1, n_lon)
    partner = n_lon - 1 - lon
    has_north, has_south = lat < n_lat - 1, lat > 0
    is_top = lat == n_lat - 1

    barrier = pltpu.get_barrier_semaphore()
    pl.semaphore_signal(barrier, inc=1, device_id={"lon": east}, device_id_type=MESH)
    pl.semaphore_signal(barrier, inc=1, device_id={"lon": west}, device_id_type=MESH)

    @pl.when(has_north)
    def _():
        pl.semaphore_signal(barrier, inc=1, device_id={"lat": lat + 1}, device_id_type=MESH)

    @pl.when(has_south)
    def _():
        pl.semaphore_signal(barrier, inc=1, device_id={"lat": lat - 1}, device_id_type=MESH)

    @pl.when(is_top)
    def _():
        pl.semaphore_signal(barrier, inc=1, device_id={"lon": partner}, device_id_type=MESH)

    def load(t, first, count, sem):
        lanes = pl.ds(LANES * t, LANES)
        part = pl.ds(first, count)
        copies = []
        for j, (src, dst) in enumerate(
            [
                (cur_hbm.at[:, :, part, lanes], st.at[t, 0:4, :, part, :]),
                (bef_hbm.at[:, :, part, lanes], st.at[t, 4:8, :, part, :]),
                (tm_hbm.at[:, part, lanes], mk.at[t, 0, :, part, :]),
                (um_hbm.at[:, part, lanes], mk.at[t, 1, :, part, :]),
                (vm_hbm.at[:, part, lanes], mk.at[t, 2, :, part, :]),
            ]
        ):
            copy = pltpu.make_async_copy(src, dst, load_sems.at[sem, t, j])
            copy.start()
            copies.append(copy)
        return copies

    early, late = [], []
    for t in ends:
        early += load(t, 0, rows, 0)
    for t in middle:
        early += load(t, rows - SUB, SUB, 1)
    for t in middle:
        late += load(t, 0, rows - SUB, 0)
    for copy in early:
        copy.wait()

    lane = lax.broadcasted_iota(jnp.int32, (SUB, LANES), 1)
    first, last = lane == 0, lane == LANES - 1
    nothing = jnp.zeros((SUB, LANES), jnp.float32)

    def masked(t, l, strip, total):
        m = [mk[t, i, l, strip, :].astype(jnp.float32) for i in range(3)]
        fm = [m[0], m[0], m[1], m[2]]
        x = [st[t, f, l, strip, :] * fm[f % 4] for f in range(8)]
        for f in range(8):
            st[t, f, l, strip, :] = x[f]
        rho = haline * x[1] - thermal * x[0]
        total = rho if total is None else total + rho
        pr[t, l, strip, :] = total - 0.5 * rho
        return x, m, total

    def strip_of(r):
        return pl.ds(pl.multiple_of(SUB * r, SUB), SUB)

    def outer_strip(r, packs):
        strip = strip_of(r)
        packs = list(packs)
        totals = {t: None for t in ends}
        for l in range(levels):
            values = {}
            for t in ends:
                x, m, totals[t] = masked(t, l, strip, totals[t])
                values[t] = x + [m[1], m[0], m[2]]
            shift = 2 * (r * levels + l)
            here = ((lane - shift + 1) & (LANES - 1)) < 2
            for f in range(11):
                both = jnp.where(lane < LANES // 2, values[0][f], values[chunks - 1][f])
                packs[f] = jnp.where(here, pltpu.roll(both, shift, 1), packs[f])
        return tuple(packs)

    packs = lax.fori_loop(0, strips, outer_strip, (nothing,) * 11)
    for f in range(11):
        own[f] = packs[f]

    def middle_strip(strip):
        for t in middle:
            total = None
            for l in range(levels):
                total = masked(t, l, strip, total)[2]

    def edge_row(to, row):
        for t in range(chunks):
            for l in range(levels):
                for f in range(8):
                    to[t, f, l : l + 1, :] = st[t, f, l, row : row + 1, :]
                for f, i in ((8, 2), (9, 0), (10, 1)):
                    mask = mk[t, i, l, row : row + 1, :].astype(jnp.float32)
                    to[t, f, l : l + 1, :] = mask

    middle_strip(slice(rows - SUB, rows))
    edge_row(top, rows - 1)

    @pl.when(has_south)
    def _():
        pl.semaphore_wait(barrier, 4)

    @pl.when(lat == 0)
    def _():
        pl.semaphore_wait(barrier, 3)

    def remote(src, dst, which, device):
        return pltpu.make_async_remote_copy(
            src_ref=src,
            dst_ref=dst,
            send_sem=send_sems.at[which],
            recv_sem=recv_sems.at[which],
            device_id=device,
            device_id_type=MESH,
        )

    to_west = remote(own.at[0:9], from_e, 0, {"lon": west})
    to_east = remote(own.at[0:9], from_w, 1, {"lon": east})
    to_north = remote(top.at[:, 0:9], from_s, 2, {"lat": lat + 1})
    to_south = remote(bottom.at[:, 0:8], from_n, 3, {"lat": lat - 1})
    to_fold = remote(top.at[:, 0:8], from_n, 4, {"lon": partner})

    @pl.when(is_top)
    def _():
        to_fold.start()

    to_west.start()
    to_east.start()

    @pl.when(has_north)
    def _():
        to_north.start()

    for copy in late:
        copy.wait()

    def middle_step(r, carry):
        middle_strip(strip_of(r))
        return carry

    lax.fori_loop(0, strips - 1, middle_step, 0)
    edge_row(bottom, 0)

    @pl.when(has_south)
    def _():
        to_south.start()

    for t in range(chunks):
        for l in range(levels):
            for f in range(8):
                st[t, f, l, rows : rows + SUB, :] = nothing
            for k in range(4):
                fn[t, k, l, 0:SUB, :] = nothing
            pr[t, l, rows : rows + SUB, :] = nothing

    advect = advect_coef * 0.5 * twice_step
    diffuse = diffuse_coef * twice_step
    push = gravity * twice_step
    keep = 1.0 - 2.0 * asselin

    def step_strip(r, carry):
        at = pl.multiple_of(SUB * r, SUB)
        strip, above = pl.ds(at, SUB), pl.ds(at + 1, SUB)
        put, below = pl.ds(at + SUB, SUB), pl.ds(at + SUB - 1, SUB)
        row = lat * rows + r * SUB + lax.broadcasted_iota(jnp.int32, (SUB, LANES), 0)
        cor = coriolis * (2.0 * (row.astype(jnp.float32) + 0.5) / (rows * n_lat) - 1.0)
        cor = twice_step * cor

        def finish(l, t, west_flux, east_flux):
            lanes = pl.ds(LANES * t, LANES)
            h = [st[t, f, l, strip, :] for f in range(8)]
            n = [st[t, f, l, above, :] for f in range(8)]
            m = [mk[t, i, l, strip, :].astype(jnp.float32) for i in range(3)]
            fm = [m[0], m[0], m[1], m[2]]
            p = pr[t, l, strip, :]
            speed, mask = advect * h[3], diffuse * m[2]
            tend = []
            for k in range(4):
                flux_n = speed * (h[k] + n[k]) - mask * (n[4 + k] - h[4 + k])
                fn[t, k, l, put, :] = flux_n
                tend.append((west_flux[k] - east_flux[k]) + (fn[t, k, l, below, :] - flux_n))
            tend[2] = tend[2] + (cor * h[3] + push * m[1] * p)
            tend[3] = tend[3] - (cor * h[2] + push * m[2] * (pr[t, l, above, :] - p))
            for k in range(4):
                after = (h[4 + k] + tend[k]) * fm[k]
                after_ref[k, l, strip, lanes] = after
                filt_ref[k, l, strip, lanes] = keep * h[k] + asselin * (h[4 + k] + after)

        for l in range(levels):
            prior_speed = jnp.full((SUB, LANES), DRY, jnp.float32)
            prior_part = [nothing] * 4
            waiting = None
            for t in range(chunks):
                h = [st[t, f, l, strip, :] for f in range(8)]
                wet = mk[t, 1, l, strip, :]
                speed, mask = advect * h[2], diffuse * wet.astype(jnp.float32)
                moved = pltpu.roll(jnp.where(wet > 0, h[2], DRY), 1, 1)
                speed_w = jnp.where(first, prior_speed, moved)
                prior_speed = moved
                dry = speed_w > 0.5 * DRY
                speed_w = jnp.where(dry, 0.0, advect * speed_w)
                mask_w = jnp.where(dry, 0.0, diffuse)
                flux_w, back = [], []
                for k in range(4):
                    part = pltpu.roll(speed * h[k] + mask * h[4 + k], 1, 1)
                    flux = jnp.where(first, prior_part[k], part)
                    prior_part[k] = part
                    flux = flux + (speed_w * h[k] - mask_w * h[4 + k])
                    if t == 0:
                        flux = jnp.where(first, 0.0, flux)
                    flux_w.append(flux)
                    carried = flux
                    if k == 2:
                        carried = flux + (push / diffuse) * mask_w * pr[t, l, strip, :]
                    back.append(pltpu.roll(carried, LANES - 1, 1))
                if waiting is not None:
                    flux_e = [jnp.where(last, y, x) for x, y in zip(waiting[1], back)]
                    finish(l, t - 1, waiting[0], flux_e)
                waiting = flux_w, back
            flux_e = [jnp.where(last, 0.0, x) for x in waiting[1]]
            finish(l, chunks - 1, waiting[0], flux_e)
        return carry

    lax.fori_loop(0, strips, step_strip, 0)

    def add_row(to_row, t, k, change):
        lanes = pl.ds(LANES * t, LANES)
        for l in range(levels):
            one = change[l : l + 1, :]
            after_ref[k, l, to_row : to_row + 1, lanes] += one
            filt_ref[k, l, to_row : to_row + 1, lanes] += asselin * one

    @pl.when(has_south)
    def _():
        to_north.wait_recv()
        for t in range(chunks):
            h = [from_s[t, f] for f in range(9)]
            a = [bottom[t, f] for f in range(11)]
            fm = [a[9], a[9], a[10], a[8]]
            speed, mask = advect * h[3], diffuse * h[8]
            for k in range(4):
                flux = speed * (h[k] + a[k]) - mask * (a[4 + k] - h[4 + k])
                add_row(0, t, k, flux * fm[k])

    to_west.wait_recv()
    to_east.wait_recv()

    even = (lane & 1) == 0
    left = [jnp.where(even, pltpu.roll(from_w[f], 1, 1), own[f]) for f in range(9)]
    right = [jnp.where(even, own[f], pltpu.roll(from_e[f], LANES - 1, 1)) for f in range(8)]
    rho = haline * right[1] - thermal * right[0]
    pres = 0.5 * rho
    level = (lane + 1) // 2 % levels
    for l in range(1, levels):
        pres = pres + jnp.where(level >= l, pltpu.roll(rho, 2 * l, 1), 0.0)
    speed, mask = advect * left[2], diffuse * left[8]
    fm = [own[9], own[9], own[8], own[10]]
    for k in range(4):
        flux = speed * (left[k] + right[k]) - mask * (right[4 + k] - left[4 + k])
        if k == 2:
            flux = jnp.where(even, flux, flux + push * left[8] * pres)
        from_e[k] = jnp.where(even, flux, -flux) * fm[k]

    def outer_add(r, carry):
        strip = strip_of(r)
        for k in range(4):
            change = from_e[k]
            for l in range(levels):
                one = pltpu.roll(change, LANES - 2 * (r * levels + l), 1)
                for t, where in ((0, first), (chunks - 1, last)):
                    lanes = pl.ds(LANES * t, LANES)
                    add = jnp.where(where, one, 0.0)
                    after_ref[k, l, strip, lanes] += add
                    filt_ref[k, l, strip, lanes] += asselin * add
        return carry

    lax.fori_loop(0, strips, outer_add, 0)

    @pl.when(has_north)
    def _():
        to_south.wait_recv()

    @pl.when(is_top)
    def _():
        to_fold.wait_recv()
        mirror = LANES - 1 - lax.broadcasted_iota(jnp.int32, (levels, LANES), 1)

        def turned(x):
            return jnp.take_along_axis(x, mirror, axis=1, mode="promise_in_bounds")

        for t in range((chunks + 1) // 2):
            for f in range(8):
                sign = 1.0 if f % 4 < 2 else -1.0
                a, b = from_n[t, f], from_n[chunks - 1 - t, f]
                from_n[t, f] = sign * turned(b)
                from_n[chunks - 1 - t, f] = sign * turned(a)

    for t in range(chunks):
        h = [top[t, f] for f in range(11)]
        a = [from_n[t, f] for f in range(8)]
        fm = [h[9], h[9], h[10], h[8]]
        speed, mask = advect * h[3], diffuse * h[8]
        rho = haline * a[1] - thermal * a[0]
        total, pres = None, []
        for l in range(levels):
            one = rho[l : l + 1, :]
            total = one if total is None else total + one
            pres.append(total - 0.5 * one)
        for k in range(4):
            change = mask * a[4 + k] - speed * a[k]
            if k == 3:
                change = change - push * h[8] * jnp.concatenate(pres, 0)
            add_row(rows - 1, t, k, change * fm[k])

    to_west.wait_send()
    to_east.wait_send()

    @pl.when(has_north)
    def _():
        to_north.wait_send()

    @pl.when(has_south)
    def _():
        to_south.wait_send()

    @pl.when(is_top)
    def _():
        to_fold.wait_send()


def shards(n_lon, n_lat, *args):
    _, levels, rows, cols = args[0].shape
    chunks = cols // LANES
    f32 = jnp.float32
    out = jax.ShapeDtypeStruct(args[0].shape, f32)
    args = [pltpu.with_memory_space_constraint(x, pltpu.HBM) for x in args]
    return pl.pallas_call(
        functools.partial(kernel, n_lon, n_lat),
        out_shape=(out, out),
        in_specs=[pl.BlockSpec(memory_space=pl.ANY)] * 5,
        out_specs=(pl.BlockSpec(memory_space=pltpu.VMEM),) * 2,
        scratch_shapes=[
            pltpu.VMEM((chunks, 8, levels, rows + SUB, LANES), f32),
            pltpu.VMEM((chunks, 3, levels, rows, LANES), jnp.int32),
            pltpu.VMEM((chunks, levels, rows + SUB, LANES), f32),
            pltpu.VMEM((chunks, 4, levels, rows + SUB, LANES), f32),
            pltpu.VMEM((11, SUB, LANES), f32),
            pltpu.VMEM((9, SUB, LANES), f32),
            pltpu.VMEM((9, SUB, LANES), f32),
            pltpu.VMEM((chunks, 11, levels, LANES), f32),
            pltpu.VMEM((chunks, 11, levels, LANES), f32),
            pltpu.VMEM((chunks, 8, levels, LANES), f32),
            pltpu.VMEM((chunks, 9, levels, LANES), f32),
            pltpu.SemaphoreType.DMA((2, chunks, 5)),
            pltpu.SemaphoreType.DMA((5,)),
            pltpu.SemaphoreType.DMA((5,)),
        ],
        compiler_params=pltpu.CompilerParams(
            collective_id=0, has_side_effects=True, vmem_limit_bytes=28 << 20
        ),
    )(*args)


def solution(mesh):
    state = P(None, None, "lat", "lon")
    flags = P(None, "lat", "lon")
    return jax.shard_map(
        functools.partial(shards, mesh.shape["lon"], mesh.shape["lat"]),
        mesh=mesh,
        in_specs=(state, state, flags, flags, flags),
        out_specs=(state, state),
        check_vma=False,
    )
```

time: 28 us -> 19.3 us (0.69); the launches traced: 27.5 us -> 19.2 us
  Pallas kernels: 24.2 us -> 15.9 us
    pallas_call x1, Pallas kernels: 24.2 us -> 15.9 us  [shards(): pl.pallas_call(functools.partial(kernel, n_lon, n_lat), out_shape=(out, o...]
where the time goes in v2:
time: 19.3 us; the launch traced here: 19.2 us
  Pallas kernels  15.9 us (82%)
  local copies, waits for them, and re-layouts  2.64 us (14%)
  between operations  0.64 us (3%)
    pallas_call x1, Pallas kernels, shards(): pl.pallas_call(functools.partial(kernel, n_lon, n_lat), out_shape=(out, o...  15.9 us
    unnamed x2, local copies, waits for them, and re-layouts  2.64 us

profile of v2, /device:TPU:26, one launch (start us, length us, event | category | flops | bytes accessed | tf_op | source)
XLA Modules:
  0.0 19.2 jit_solution(14969128457972652349)
XLA Ops:
  0.6 15.9 %shard_map.68 = (f32[4,4,64,512]{3,2,1,0:T(8,128)S(1)}, f32[4,4,64,512]{3,2,1,0:T(8,128)S(1)}) custom-call(f32[4,4,64,512]{3,2,1,0:T(8,128)} %bef_hbm.1, f32[4,4,64,512]{3,2,1,0:T(8,128)} %cur_hbm.1, s32[4,64,512]{2,1,0:T(8,128)} %tm_hbm.1, s32[4,64,512]{2,1,0:T(8,128)} %um_hbm.1, s32[4,64,512]{2,1,0:T(8,128)} %vm_hbm.1), custom_call_target="tpu_custom_call" | custom-call | tf_op jit(solution)/shard_map/pallas_call | solution.py:399
  16.6 1.3 %copy.9 = f32[4,4,64,512]{3,2,1,0:T(8,128)} copy(f32[4,4,64,512]{3,2,1,0:T(8,128)S(1)} %get-tuple-element.4) | data formatting | bytes 4194304
  17.9 1.3 %copy.10 = f32[4,4,64,512]{3,2,1,0:T(8,128)} copy(f32[4,4,64,512]{3,2,1,0:T(8,128)S(1)} %get-tuple-element.5) | data formatting | bytes 4194304

commit v3 on v2

--- a/solution.py
+++ b/solution.py
@@ -20,6 +20,7 @@
 SUB = 8
 MESH = pl.DeviceIdType.MESH
 DRY = 1e30
+PIECES = 4
 
 
 def kernel(
@@ -32,6 +33,9 @@
     vm_hbm,
     after_ref,
     filt_ref,
+    outer_ref,
+    south_ref,
+    north_ref,
     st,
     mk,
     pr,
@@ -92,15 +96,16 @@
             copies.append(copy)
         return copies
 
-    early, late = [], []
-    for t in ends:
-        early += load(t, 0, rows, 0)
+    piece = rows // PIECES
+    highest, outer, late = [], [], []
     for t in middle:
-        early += load(t, rows - SUB, SUB, 1)
+        highest += load(t, rows - SUB, SUB, PIECES)
+    for i in range(PIECES):
+        outer.append([])
+        for t in ends:
+            outer[i] += load(t, i * piece, piece, i)
     for t in middle:
         late += load(t, 0, rows - SUB, 0)
-    for copy in early:
-        copy.wait()
 
     lane = lax.broadcasted_iota(jnp.int32, (SUB, LANES), 1)
     first, last = lane == 0, lane == LANES - 1
@@ -128,17 +133,26 @@
             values = {}
             for t in ends:
                 x, m, totals[t] = masked(t, l, strip, totals[t])
-                values[t] = x + [m[1], m[0], m[2]]
+                values[t] = x + [m[1]]
             shift = 2 * (r * levels + l)
             here = ((lane - shift + 1) & (LANES - 1)) < 2
-            for f in range(11):
+            for f in range(9):
                 both = jnp.where(lane < LANES // 2, values[0][f], values[chunks - 1][f])
                 packs[f] = jnp.where(here, pltpu.roll(both, shift, 1), packs[f])
         return tuple(packs)
 
-    packs = lax.fori_loop(0, strips, outer_strip, (nothing,) * 11)
-    for f in range(11):
-        own[f] = packs[f]
+    def outer_flags(r, packs):
+        strip = strip_of(r)
+        packs = list(packs)
+        for l in range(levels):
+            shift = 2 * (r * levels + l)
+            here = ((lane - shift + 1) & (LANES - 1)) < 2
+            for f, i in enumerate((0, 2)):
+                both = jnp.where(
+                    lane < LANES // 2, mk[0, i, l, strip, :], mk[chunks - 1, i, l, strip, :]
+                ).astype(jnp.float32)
+                packs[f] = jnp.where(here, pltpu.roll(both, shift, 1), packs[f])
+        return tuple(packs)
 
     def middle_strip(strip):
         for t in middle:
@@ -155,7 +169,16 @@
                     mask = mk[t, i, l, row : row + 1, :].astype(jnp.float32)
                     to[t, f, l : l + 1, :] = mask
 
+    for copy in highest:
+        copy.wait()
     middle_strip(slice(rows - SUB, rows))
+    packs = (nothing,) * 9
+    for i in range(PIECES):
+        for copy in outer[i]:
+            copy.wait()
+        packs = lax.fori_loop(i * piece // SUB, (i + 1) * piece // SUB, outer_strip, packs)
+    for f in range(9):
+        own[f] = packs[f]
     edge_row(top, rows - 1)
 
     @pl.when(has_south)
@@ -202,6 +225,7 @@
 
     lax.fori_loop(0, strips - 1, middle_step, 0)
     edge_row(bottom, 0)
+    own[9], own[10] = lax.fori_loop(0, strips, outer_flags, (nothing,) * 2)
 
     @pl.when(has_south)
     def _():
@@ -285,13 +309,6 @@
 
     lax.fori_loop(0, strips, step_strip, 0)
 
-    def add_row(to_row, t, k, change):
-        lanes = pl.ds(LANES * t, LANES)
-        for l in range(levels):
-            one = change[l : l + 1, :]
-            after_ref[k, l, to_row : to_row + 1, lanes] += one
-            filt_ref[k, l, to_row : to_row + 1, lanes] += asselin * one
-
     @pl.when(has_south)
     def _():
         to_north.wait_recv()
@@ -302,7 +319,11 @@
             speed, mask = advect * h[3], diffuse * h[8]
             for k in range(4):
                 flux = speed * (h[k] + a[k]) - mask * (a[4 + k] - h[4 + k])
-                add_row(0, t, k, flux * fm[k])
+                south_ref[t, k] = flux * fm[k]
+
+    @pl.when(lat == 0)
+    def _():
+        south_ref[...] = jnp.zeros(south_ref.shape, jnp.float32)
 
     to_west.wait_recv()
     to_east.wait_recv()
@@ -321,22 +342,7 @@
         flux = speed * (left[k] + right[k]) - mask * (right[4 + k] - left[4 + k])
         if k == 2:
             flux = jnp.where(even, flux, flux + push * left[8] * pres)
-        from_e[k] = jnp.where(even, flux, -flux) * fm[k]
-
-    def outer_add(r, carry):
-        strip = strip_of(r)
-        for k in range(4):
-            change = from_e[k]
-            for l in range(levels):
-                one = pltpu.roll(change, LANES - 2 * (r * levels + l), 1)
-                for t, where in ((0, first), (chunks - 1, last)):
-                    lanes = pl.ds(LANES * t, LANES)
-                    add = jnp.where(where, one, 0.0)
-                    after_ref[k, l, strip, lanes] += add
-                    filt_ref[k, l, strip, lanes] += asselin * add
-        return carry
-
-    lax.fori_loop(0, strips, outer_add, 0)
+        outer_ref[k] = jnp.where(even, flux, -flux) * fm[k]
 
     @pl.when(has_north)
     def _():
@@ -372,7 +378,7 @@
             change = mask * a[4 + k] - speed * a[k]
             if k == 3:
                 change = change - push * h[8] * jnp.concatenate(pres, 0)
-            add_row(rows - 1, t, k, change * fm[k])
+            north_ref[t, k] = change * fm[k]
 
     to_west.wait_send()
     to_east.wait_send()
@@ -388,6 +394,92 @@
     @pl.when(is_top)
     def _():
         to_fold.wait_send()
+
+
+def closing_kernel(
+    after_ref,
+    filt_ref,
+    outer_ref,
+    south_ref,
+    north_ref,
+    after_hbm,
+    filt_hbm,
+    edge,
+    ribbon,
+    sems,
+):
+    _, levels, rows, cols = after_ref.shape
+    chunks = cols // LANES
+    strips = rows // SUB
+    blocks, targets = (after_ref, filt_ref), (after_hbm, filt_hbm)
+    copies = []
+
+    def store(src, dst):
+        copy = pltpu.make_async_copy(src, dst, sems.at[len(copies)])
+        copy.start()
+        copies.append(copy)
+
+    inner_lanes = pl.ds(LANES, cols - 2 * LANES)
+    inner_rows = pl.ds(SUB, rows - 2 * SUB)
+    for src, dst in zip(blocks, targets):
+        place = (slice(None), slice(None), inner_rows, inner_lanes)
+        store(src.at[place], dst.at[place])
+
+    lane = lax.broadcasted_iota(jnp.int32, (SUB, LANES), 1)
+    sub = lax.broadcasted_iota(jnp.int32, (SUB, LANES), 0)
+    sides = ((south_ref, 0, 0), (north_ref, rows - SUB, SUB - 1))
+
+    def row_change(ref, t, k, l, where):
+        one = jnp.broadcast_to(ref[t, k, l : l + 1, :], (SUB, LANES))
+        return jnp.where(sub == where, one, 0.0)
+
+    for i, (ref, row, where) in enumerate(sides):
+        for k in range(4):
+            for l in range(levels):
+                for t in range(1, chunks - 1):
+                    lanes = pl.ds(LANES * t, LANES)
+                    change = row_change(ref, t, k, l, where)
+                    to = pl.ds(LANES * (t - 1), LANES)
+                    ribbon[0, i, k, l, :, to] = after_ref[k, l, row : row + SUB, lanes] + change
+                    ribbon[1, i, k, l, :, to] = (
+                        filt_ref[k, l, row : row + SUB, lanes] + asselin * change
+                    )
+        for o in range(2):
+            store(ribbon.at[o, i], targets[o].at[:, :, pl.ds(row, SUB), inner_lanes])
+
+    def outer_strip(r, carry):
+        strip = pl.ds(pl.multiple_of(SUB * r, SUB), SUB)
+        for k in range(4):
+            for l in range(levels):
+                one = pltpu.roll(outer_ref[k], LANES - 2 * (r * levels + l), 1)
+                for i, (t, where) in enumerate(((0, 0), (chunks - 1, LANES - 1))):
+                    lanes = pl.ds(LANES * t, LANES)
+                    change = jnp.where(lane == where, one, 0.0)
+                    edge[0, i, k, l, strip, :] = after_ref[k, l, strip, lanes] + change
+                    edge[1, i, k, l, strip, :] = filt_ref[k, l, strip, lanes] + asselin * change
+        return carry
+
+    piece = rows // PIECES
+    for part in range(PIECES):
+        lax.fori_loop(part * piece // SUB, (part + 1) * piece // SUB, outer_strip, 0)
+        for ref, row, where in sides:
+            if part * piece <= row < (part + 1) * piece:
+                for k in range(4):
+                    for l in range(levels):
+                        for i, t in enumerate((0, chunks - 1)):
+                            change = row_change(ref, t, k, l, where)
+                            edge[0, i, k, l, row : row + SUB, :] += change
+                            edge[1, i, k, l, row : row + SUB, :] += asselin * change
+        span = pl.ds(part * piece, piece)
+        for o in range(2):
+            for i, t in enumerate((0, chunks - 1)):
+                store(
+                    edge.at[o, i, :, :, span, :],
+                    targets[o].at[:, :, span, pl.ds(LANES * t, LANES)],
+                )
+
+    for copy in copies:
+        copy.wait()
 
 
 def shards(n_lon, n_lat, *args):
@@ -396,11 +488,18 @@
     f32 = jnp.float32
     out = jax.ShapeDtypeStruct(args[0].shape, f32)
     args = [pltpu.with_memory_space_constraint(x, pltpu.HBM) for x in args]
-    return pl.pallas_call(
+    block = pl.BlockSpec(memory_space=pltpu.VMEM)
+    parts = pl.pallas_call(
         functools.partial(kernel, n_lon, n_lat),
-        out_shape=(out, out),
+        out_shape=(
+            out,
+            out,
+            jax.ShapeDtypeStruct((4, SUB, LANES), f32),
+            jax.ShapeDtypeStruct((chunks, 4, levels, LANES), f32),
+            jax.ShapeDtypeStruct((chunks, 4, levels, LANES), f32),
+        ),
         in_specs=[pl.BlockSpec(memory_space=pl.ANY)] * 5,
-        out_specs=(pl.BlockSpec(memory_space=pltpu.VMEM),) * 2,
+        out_specs=(block,) * 5,
         scratch_shapes=[
             pltpu.VMEM((chunks, 8, levels, rows + SUB, LANES), f32),
             pltpu.VMEM((chunks, 3, levels, rows, LANES), jnp.int32),
@@ -413,7 +512,7 @@
             pltpu.VMEM((chunks, 11, levels, LANES), f32),
             pltpu.VMEM((chunks, 8, levels, LANES), f32),
             pltpu.VMEM((chunks, 9, levels, LANES), f32),
-            pltpu.SemaphoreType.DMA((2, chunks, 5)),
+            pltpu.SemaphoreType.DMA((PIECES + 1, chunks, 5)),
             pltpu.SemaphoreType.DMA((5,)),
             pltpu.SemaphoreType.DMA((5,)),
         ],
@@ -421,6 +520,19 @@
             collective_id=0, has_side_effects=True, vmem_limit_bytes=28 << 20
         ),
     )(*args)
+    parts = [pltpu.with_memory_space_constraint(x, pltpu.VMEM) for x in parts]
+    return pl.pallas_call(
+        closing_kernel,
+        out_shape=(out, out),
+        in_specs=[block] * 5,
+        out_specs=(pl.BlockSpec(memory_space=pl.ANY),) * 2,
+        scratch_shapes=[
+            pltpu.VMEM((2, 2, 4, levels, rows, LANES), f32),
+            pltpu.VMEM((2, 2, 4, levels, SUB, cols - 2 * LANES), f32),
+            pltpu.SemaphoreType.DMA((6 + 4 * PIECES,)),
+        ],
+        compiler_params=pltpu.CompilerParams(vmem_limit_bytes=28 << 20),
+    )(*parts)
 
 
 def solution(mesh):

time: 19.3 us -> 18.1 us (0.938)
  local copies, waits for them, and re-layouts: 2.64 us -> 0 us
  Pallas kernels: 15.9 us -> 17.2 us
    unnamed x2 -> x0, local copies, waits for them, and re-layouts: 2.64 us -> none
    pallas_call x0 -> x1, Pallas kernels: none -> 2.19 us  [shards(): pl.pallas_call(closing_kernel, out_shape=(out, out), in_specs=[block] * 5...]
    pallas_call x1, Pallas kernels: 15.9 us -> 15 us  [shards(): pl.pallas_call(functools.partial(kernel, n_lon, n_lat), out_shape=(out, o...]
where the time goes in v3:
time: 18.1 us; the launch traced here: 17.9 us
  Pallas kernels  17.2 us (95%)
  between operations  0.64 us (4%)
    pallas_call x1, Pallas kernels, shards(): pl.pallas_call(functools.partial(kernel, n_lon, n_lat), out_shape=(out, o...  15 us
    pallas_call x1, Pallas kernels, shards(): pl.pallas_call(closing_kernel, out_shape=(out, out), in_specs=[block] * 5...  2.19 us

profile of v3, /device:TPU:26, one launch (start us, length us, event | category | flops | bytes accessed | tf_op | source)
XLA Modules:
  0.0 17.9 jit_solution(7902745348274088195)
XLA Ops:
  0.6 15.0 %shard_map.68 = (f32[4,4,64,512]{3,2,1,0:T(8,128)S(1)}, f32[4,4,64,512]{3,2,1,0:T(8,128)S(1)}, f32[4,8,128]{2,1,0:T(8,128)S(1)}, f32[4,4,4,128]{3,2,1,0:T(4,128)S(1)}, f32[4,4,4,128]{3,2,1,0:T(4,128)S(1)}) custom-call(f32[4,4,64,512]{3,2,1,0:T(8,128)} %bef_hbm.1, f32[4,4,64,512]{3,2,1,0:T(8,128)} %cur_hbm.1, s32[4,64,512]{2,1,0:T(8,128)} %tm_hbm.1, ...), custom_call_target="tpu_custom_call" | custom-call | tf_op jit(solution)/shard_map/pallas_call | solution.py:492
  15.7 2.2 %shard_map.69 = (f32[4,4,64,512]{3,2,1,0:T(8,128)}, f32[4,4,64,512]{3,2,1,0:T(8,128)}) custom-call(f32[4,4,64,512]{3,2,1,0:T(8,128)S(1)} %get-tuple-element.7.after_ref, f32[4,4,64,512]{3,2,1,0:T(8,128)S(1)} %get-tuple-element.8.filt_ref, f32[4,8,128]{2,1,0:T(8,128)S(1)} %get-tuple-element.9.outer_ref, f32[4,4,4,128]{3,2,1,0:T(4,128)S(1)} %get-tuple-element.10.south_ref, ...), custom_call_target="tpu_custom_call" | custom-call | tf_op jit(solution)/shard_map/pallas_call | solution.py:524

commit v4 on v3

--- a/solution.py
+++ b/solution.py
@@ -40,7 +40,11 @@
     mk,
     pr,
     fn,
-    own,
+    raw,
+    raw_flags,
+    own_e,
+    own_w,
+    flags,
     from_e,
     from_w,
     top,
@@ -55,17 +59,25 @@
     chunks = cols // LANES
     strips = rows // SUB
     middle = range(1, chunks - 1)
-    ends = sorted({0, chunks - 1})
+    high = rows - SUB
     lon, lat = lax.axis_index("lon"), lax.axis_index("lat")
     east, west = lax.rem(lon + 1, n_lon), lax.rem(lon + n_lon - 1, n_lon)
     partner = n_lon - 1 - lon
     has_north, has_south = lat < n_lat - 1, lat > 0
     is_top = lat == n_lat - 1
+    across = lax.rem(lon, n_lon // 2)
+    sends_last = jnp.logical_and(is_top, across < n_lon // 4)
+    sends_first = jnp.logical_not(sends_last)
+    answers = across == 0
+    starts = jnp.logical_not(answers)
 
     barrier = pltpu.get_barrier_semaphore()
-    pl.semaphore_signal(barrier, inc=1, device_id={"lon": east}, device_id_type=MESH)
     pl.semaphore_signal(barrier, inc=1, device_id={"lon": west}, device_id_type=MESH)
 
+    @pl.when(across != n_lon // 2 - 1)
+    def _():
+        pl.semaphore_signal(barrier, inc=1, device_id={"lon": east}, device_id_type=MESH)
+
     @pl.when(has_north)
     def _():
         pl.semaphore_signal(barrier, inc=1, device_id={"lat": lat + 1}, device_id_type=MESH)
@@ -78,43 +90,58 @@
     def _():
         pl.semaphore_signal(barrier, inc=1, device_id={"lon": partner}, device_id_type=MESH)
 
-    def load(t, first, count, sem):
+    def load(sem, pairs):
+        copies = []
+        for i, (src, dst) in enumerate(pairs):
+            copy = pltpu.make_async_copy(src, dst, load_sems.at[sem, i])
+            copy.start()
+            copies.append(copy)
+        return copies
+
+    def load_tiles(sem, t, begin, end):
         lanes = pl.ds(LANES * t, LANES)
-        part = pl.ds(first, count)
-        copies = []
-        for j, (src, dst) in enumerate(
+        part = pl.ds(begin, end - begin)
+        return load(
+            sem,
             [
                 (cur_hbm.at[:, :, part, lanes], st.at[t, 0:4, :, part, :]),
                 (bef_hbm.at[:, :, part, lanes], st.at[t, 4:8, :, part, :]),
                 (tm_hbm.at[:, part, lanes], mk.at[t, 0, :, part, :]),
                 (um_hbm.at[:, part, lanes], mk.at[t, 1, :, part, :]),
                 (vm_hbm.at[:, part, lanes], mk.at[t, 2, :, part, :]),
-            ]
-        ):
-            copy = pltpu.make_async_copy(src, dst, load_sems.at[sem, t, j])
-            copy.start()
-            copies.append(copy)
-        return copies
-
-    piece = rows // PIECES
-    highest, outer, late = [], [], []
-    for t in middle:
-        highest += load(t, rows - SUB, SUB, PIECES)
-    for i in range(PIECES):
-        outer.append([])
-        for t in ends:
-            outer[i] += load(t, i * piece, piece, i)
-    for t in middle:
-        late += load(t, 0, rows - SUB, 0)
+            ],
+        )
+
+    part = pl.ds(high, SUB)
+    highest = load(
+        0,
+        [
+            (cur_hbm.at[:, :, part, :], raw.at[0:4]),
+            (bef_hbm.at[:, :, part, :], raw.at[4:8]),
+            (tm_hbm.at[:, part, :], raw_flags.at[0]),
+            (um_hbm.at[:, part, :], raw_flags.at[1]),
+            (vm_hbm.at[:, part, :], raw_flags.at[2]),
+        ],
+    )
+    half = strips // 2
+    eastern = [
+        load_tiles(1, chunks - 1, 0, SUB * half),
+        load_tiles(2, chunks - 1, SUB * half, high),
+    ]
+
+    greetings = 3 + has_south.astype(jnp.int32) - answers.astype(jnp.int32)
 
     lane = lax.broadcasted_iota(jnp.int32, (SUB, LANES), 1)
     first, last = lane == 0, lane == LANES - 1
     nothing = jnp.zeros((SUB, LANES), jnp.float32)
 
-    def masked(t, l, strip, total):
-        m = [mk[t, i, l, strip, :].astype(jnp.float32) for i in range(3)]
+    def masked(t, l, strip, total, x=None, m=None):
+        if x is None:
+            x = [st[t, f, l, strip, :] for f in range(8)]
+            m = [mk[t, i, l, strip, :] for i in range(3)]
+        m = [y.astype(jnp.float32) for y in m]
         fm = [m[0], m[0], m[1], m[2]]
-        x = [st[t, f, l, strip, :] * fm[f % 4] for f in range(8)]
+        x = [x[f] * fm[f % 4] for f in range(8)]
         for f in range(8):
             st[t, f, l, strip, :] = x[f]
         rho = haline * x[1] - thermal * x[0]
@@ -125,20 +152,24 @@
     def strip_of(r):
         return pl.ds(pl.multiple_of(SUB * r, SUB), SUB)
 
-    def outer_strip(r, packs):
-        strip = strip_of(r)
-        packs = list(packs)
-        totals = {t: None for t in ends}
+    def pack(packs, values, shift, place):
+        here = lane == ((shift + place) & (LANES - 1))
+        return [
+            jnp.where(here, pltpu.roll(x, shift, 1), old) for x, old in zip(values, packs)
+        ]
+
+    def eastern_strip(r, packs):
+        total = None
         for l in range(levels):
-            values = {}
-            for t in ends:
-                x, m, totals[t] = masked(t, l, strip, totals[t])
-                values[t] = x + [m[1]]
-            shift = 2 * (r * levels + l)
-            here = ((lane - shift + 1) & (LANES - 1)) < 2
-            for f in range(9):
-                both = jnp.where(lane < LANES // 2, values[0][f], values[chunks - 1][f])
-                packs[f] = jnp.where(here, pltpu.roll(both, shift, 1), packs[f])
+            x, m, total = masked(chunks - 1, l, strip_of(r), total)
+            packs = pack(packs, x + [m[1]], 2 * (r * levels + l), -1)
+        return tuple(packs)
+
+    def western_strip(r, packs):
+        total = None
+        for l in range(levels):
+            x, m, total = masked(0, l, strip_of(r), total)
+            packs = pack(packs, x, 2 * (r * levels + l), 0)
         return tuple(packs)
 
     def outer_flags(r, packs):
@@ -147,11 +178,11 @@
         for l in range(levels):
             shift = 2 * (r * levels + l)
             here = ((lane - shift + 1) & (LANES - 1)) < 2
-            for f, i in enumerate((0, 2)):
+            for i in range(3):
                 both = jnp.where(
                     lane < LANES // 2, mk[0, i, l, strip, :], mk[chunks - 1, i, l, strip, :]
                 ).astype(jnp.float32)
-                packs[f] = jnp.where(here, pltpu.roll(both, shift, 1), packs[f])
+                packs[i] = jnp.where(here, pltpu.roll(both, shift, 1), packs[i])
         return tuple(packs)
 
     def middle_strip(strip):
@@ -168,26 +199,6 @@
                 for f, i in ((8, 2), (9, 0), (10, 1)):
                     mask = mk[t, i, l, row : row + 1, :].astype(jnp.float32)
                     to[t, f, l : l + 1, :] = mask
-
-    for copy in highest:
-        copy.wait()
-    middle_strip(slice(rows - SUB, rows))
-    packs = (nothing,) * 9
-    for i in range(PIECES):
-        for copy in outer[i]:
-            copy.wait()
-        packs = lax.fori_loop(i * piece // SUB, (i + 1) * piece // SUB, outer_strip, packs)
-    for f in range(9):
-        own[f] = packs[f]
-    edge_row(top, rows - 1)
-
-    @pl.when(has_south)
-    def _():
-        pl.semaphore_wait(barrier, 4)
-
-    @pl.when(lat == 0)
-    def _():
-        pl.semaphore_wait(barrier, 3)
 
     def remote(src, dst, which, device):
         return pltpu.make_async_remote_copy(
@@ -199,37 +210,93 @@
             device_id_type=MESH,
         )
 
-    to_west = remote(own.at[0:9], from_e, 0, {"lon": west})
-    to_east = remote(own.at[0:9], from_w, 1, {"lon": east})
+    to_west = remote(own_w, from_e, 0, {"lon": west})
+    to_east = remote(own_e, from_w, 1, {"lon": east})
     to_north = remote(top.at[:, 0:9], from_s, 2, {"lat": lat + 1})
     to_south = remote(bottom.at[:, 0:8], from_n, 3, {"lat": lat - 1})
-    to_fold = remote(top.at[:, 0:8], from_n, 4, {"lon": partner})
-
-    @pl.when(is_top)
-    def _():
-        to_fold.start()
-
-    to_west.start()
-    to_east.start()
+    to_fold = [
+        remote(top.at[t, 0:8], from_n.at[t], 4 + t, {"lon": partner}) for t in range(chunks)
+    ]
+
+    for copy in highest:
+        copy.wait()
+    top_strip = slice(high, rows)
+    for t in range(chunks):
+        lanes = slice(LANES * t, LANES * (t + 1))
+        total = None
+        for l in range(levels):
+            m = [raw_flags[i, l, :, lanes] for i in range(3)]
+            for i in range(3):
+                mk[t, i, l, top_strip, :] = m[i]
+            x = [raw[f, l, :, lanes] for f in range(8)]
+            total = masked(t, l, top_strip, total, x, m)[2]
+    edge_row(top, rows - 1)
+
+    @pl.when(jnp.logical_and(is_top, sends_first))
+    def _():
+        pl.semaphore_wait(barrier, greetings)
+        for copy in to_fold:
+            copy.start()
+
+    packs = [nothing] * 9
+    for l in range(levels):
+        x = [st[chunks - 1, f, l, top_strip, :] for f in range(8)]
+        x.append(mk[chunks - 1, 1, l, top_strip, :].astype(jnp.float32))
+        packs = pack(packs, x, 2 * ((strips - 1) * levels + l), -1)
+    packs = tuple(packs)
+    for copy in eastern[0]:
+        copy.wait()
+    packs = lax.fori_loop(0, half, eastern_strip, packs)
+    for copy in eastern[1]:
+        copy.wait()
+    western = load_tiles(3, 0, 0, high)
+    inner = [load_tiles(3 + t, t, 0, high) for t in middle]
+    packs = lax.fori_loop(half, strips - 1, eastern_strip, packs)
+    for f in range(9):
+        own_e[f] = packs[f]
 
     @pl.when(has_north)
     def _():
+        pl.semaphore_wait(barrier, greetings)
+
+    @pl.when(sends_first)
+    def _():
+        to_east.start()
+
+    @pl.when(has_north)
+    def _():
         to_north.start()
 
-    for copy in late:
+    packs = [nothing] * 8
+    for l in range(levels):
+        x = [st[0, f, l, top_strip, :] for f in range(8)]
+        packs = pack(packs, x, 2 * ((strips - 1) * levels + l), 0)
+    for copy in western:
         copy.wait()
+    packs = lax.fori_loop(0, strips - 1, western_strip, tuple(packs))
+    for f in range(8):
+        own_w[f] = packs[f]
+    @pl.when(jnp.logical_and(sends_first, starts))
+    def _():
+        to_west.start()
 
     def middle_step(r, carry):
         middle_strip(strip_of(r))
         return carry
 
+    for copies in inner:
+        for copy in copies:
+            copy.wait()
     lax.fori_loop(0, strips - 1, middle_step, 0)
     edge_row(bottom, 0)
-    own[9], own[10] = lax.fori_loop(0, strips, outer_flags, (nothing,) * 2)
-
-    @pl.when(has_south)
+
+    @pl.when(jnp.logical_and(sends_first, has_south))
     def _():
         to_south.start()
+
+    packs = lax.fori_loop(0, strips, outer_flags, (nothing,) * 3)
+    for i in range(3):
+        flags[i] = packs[i]
 
     for t in range(chunks):
         for l in range(levels):
@@ -309,6 +376,18 @@
 
     lax.fori_loop(0, strips, step_strip, 0)
 
+    @pl.when(sends_last)
+    def _():
+        pl.semaphore_wait(barrier, greetings)
+        for copy in to_fold:
+            copy.start()
+        to_south.start()
+        to_east.start()
+
+    @pl.when(jnp.logical_and(sends_last, starts))
+    def _():
+        to_west.start()
+
     @pl.when(has_south)
     def _():
         to_north.wait_recv()
@@ -325,19 +404,24 @@
     def _():
         south_ref[...] = jnp.zeros(south_ref.shape, jnp.float32)
 
+    to_east.wait_recv()
+
+    @pl.when(answers)
+    def _():
+        to_west.start()
+
     to_west.wait_recv()
-    to_east.wait_recv()
 
     even = (lane & 1) == 0
-    left = [jnp.where(even, pltpu.roll(from_w[f], 1, 1), own[f]) for f in range(9)]
-    right = [jnp.where(even, own[f], pltpu.roll(from_e[f], LANES - 1, 1)) for f in range(8)]
+    left = [jnp.where(even, pltpu.roll(from_w[f], 1, 1), own_e[f]) for f in range(9)]
+    right = [jnp.where(even, own_w[f], pltpu.roll(from_e[f], LANES - 1, 1)) for f in range(8)]
     rho = haline * right[1] - thermal * right[0]
     pres = 0.5 * rho
     level = (lane + 1) // 2 % levels
     for l in range(1, levels):
         pres = pres + jnp.where(level >= l, pltpu.roll(rho, 2 * l, 1), 0.0)
     speed, mask = advect * left[2], diffuse * left[8]
-    fm = [own[9], own[9], own[8], own[10]]
+    fm = [flags[0], flags[0], flags[1], flags[2]]
     for k in range(4):
         flux = speed * (left[k] + right[k]) - mask * (right[4 + k] - left[4 + k])
         if k == 2:
@@ -350,7 +434,8 @@
 
     @pl.when(is_top)
     def _():
-        to_fold.wait_recv()
+        for copy in to_fold:
+            copy.wait_recv()
         mirror = LANES - 1 - lax.broadcasted_iota(jnp.int32, (levels, LANES), 1)
 
         def turned(x):
@@ -393,7 +478,8 @@
 
     @pl.when(is_top)
     def _():
-        to_fold.wait_send()
+        for copy in to_fold:
+            copy.wait_send()
 
 
 def closing_kernel(
@@ -505,16 +591,20 @@
             pltpu.VMEM((chunks, 3, levels, rows, LANES), jnp.int32),
             pltpu.VMEM((chunks, levels, rows + SUB, LANES), f32),
             pltpu.VMEM((chunks, 4, levels, rows + SUB, LANES), f32),
-            pltpu.VMEM((11, SUB, LANES), f32),
+            pltpu.VMEM((8, levels, SUB, cols), f32),
+            pltpu.VMEM((3, levels, SUB, cols), jnp.int32),
             pltpu.VMEM((9, SUB, LANES), f32),
+            pltpu.VMEM((8, SUB, LANES), f32),
+            pltpu.VMEM((3, SUB, LANES), f32),
+            pltpu.VMEM((8, SUB, LANES), f32),
             pltpu.VMEM((9, SUB, LANES), f32),
             pltpu.VMEM((chunks, 11, levels, LANES), f32),
             pltpu.VMEM((chunks, 11, levels, LANES), f32),
             pltpu.VMEM((chunks, 8, levels, LANES), f32),
             pltpu.VMEM((chunks, 9, levels, LANES), f32),
-            pltpu.SemaphoreType.DMA((PIECES + 1, chunks, 5)),
-            pltpu.SemaphoreType.DMA((5,)),
-            pltpu.SemaphoreType.DMA((5,)),
+            pltpu.SemaphoreType.DMA((chunks + 2, 5)),
+            pltpu.SemaphoreType.DMA((4 + chunks,)),
+            pltpu.SemaphoreType.DMA((4 + chunks,)),
         ],
         compiler_params=pltpu.CompilerParams(
             collective_id=0, has_side_effects=True, vmem_limit_bytes=28 << 20

time: 18.1 us -> 17.4 us (0.961)
  Pallas kernels: 17.2 us -> 16.6 us
    pallas_call x1, Pallas kernels: 15 us -> 14.5 us  [shards(): pl.pallas_call(functools.partial(kernel, n_lon, n_lat), out_shape=(out, o...]
where the time goes in v4:
time: 17.4 us; the launch traced here: 17.3 us
  Pallas kernels  16.6 us (95%)
  between operations  0.64 us (4%)
    pallas_call x1, Pallas kernels, shards(): pl.pallas_call(functools.partial(kernel, n_lon, n_lat), out_shape=(out, o...  14.5 us
    pallas_call x1, Pallas kernels, shards(): pl.pallas_call(closing_kernel, out_shape=(out, out), in_specs=[block] * 5...  2.19 us

profile of v4, /device:TPU:26, one launch (start us, length us, event | category | flops | bytes accessed | tf_op | source)
XLA Modules:
  0.0 17.3 jit_solution(2407063902205433473)
XLA Ops:
  0.6 14.5 %shard_map.68 = (f32[4,4,64,512]{3,2,1,0:T(8,128)S(1)}, f32[4,4,64,512]{3,2,1,0:T(8,128)S(1)}, f32[4,8,128]{2,1,0:T(8,128)S(1)}, f32[4,4,4,128]{3,2,1,0:T(4,128)S(1)}, f32[4,4,4,128]{3,2,1,0:T(4,128)S(1)}) custom-call(f32[4,4,64,512]{3,2,1,0:T(8,128)} %bef_hbm.1, f32[4,4,64,512]{3,2,1,0:T(8,128)} %cur_hbm.1, s32[4,64,512]{2,1,0:T(8,128)} %tm_hbm.1, ...), custom_call_target="tpu_custom_call" | custom-call | tf_op jit(solution)/shard_map/pallas_call | solution.py:578
  15.1 2.2 %shard_map.69 = (f32[4,4,64,512]{3,2,1,0:T(8,128)}, f32[4,4,64,512]{3,2,1,0:T(8,128)}) custom-call(f32[4,4,64,512]{3,2,1,0:T(8,128)S(1)} %get-tuple-element.7.after_ref, f32[4,4,64,512]{3,2,1,0:T(8,128)S(1)} %get-tuple-element.8.filt_ref, f32[4,8,128]{2,1,0:T(8,128)S(1)} %get-tuple-element.9.outer_ref, f32[4,4,4,128]{3,2,1,0:T(4,128)S(1)} %get-tuple-element.10.south_ref, ...), custom_call_target="tpu_custom_call" | custom-call | tf_op jit(solution)/shard_map/pallas_call | solution.py:614

commit v5 on v4

--- a/solution.py
+++ b/solution.py
@@ -66,7 +66,7 @@
     has_north, has_south = lat < n_lat - 1, lat > 0
     is_top = lat == n_lat - 1
     across = lax.rem(lon, n_lon // 2)
-    sends_last = jnp.logical_and(is_top, across < n_lon // 4)
+    sends_last = jnp.logical_and(is_top, across < 3 * n_lon // 16)
     sends_first = jnp.logical_not(sends_last)
     answers = across == 0
     starts = jnp.logical_not(answers)
@@ -152,37 +152,38 @@
     def strip_of(r):
         return pl.ds(pl.multiple_of(SUB * r, SUB), SUB)
 
-    def pack(packs, values, shift, place):
-        here = lane == ((shift + place) & (LANES - 1))
-        return [
-            jnp.where(here, pltpu.roll(x, shift, 1), old) for x, old in zip(values, packs)
-        ]
+    group = LANES // 4
+
+    def pack(packs, values, c, source):
+        packs = list(packs)
+        for f, x in values:
+            place = group * (f % 4) + c
+            moved = pltpu.roll(x, (place - source) & (LANES - 1), 1)
+            packs[f // 4] = jnp.where(lane == place, moved, packs[f // 4])
+        return packs
 
     def eastern_strip(r, packs):
         total = None
         for l in range(levels):
             x, m, total = masked(chunks - 1, l, strip_of(r), total)
-            packs = pack(packs, x + [m[1]], 2 * (r * levels + l), -1)
+            packs = pack(packs, enumerate(x + [m[1]]), r * levels + l, LANES - 1)
         return tuple(packs)
 
     def western_strip(r, packs):
         total = None
         for l in range(levels):
             x, m, total = masked(0, l, strip_of(r), total)
-            packs = pack(packs, x, 2 * (r * levels + l), 0)
+            packs = pack(packs, enumerate(x), r * levels + l, 0)
         return tuple(packs)
 
     def outer_flags(r, packs):
         strip = strip_of(r)
         packs = list(packs)
         for l in range(levels):
-            shift = 2 * (r * levels + l)
-            here = ((lane - shift + 1) & (LANES - 1)) < 2
-            for i in range(3):
-                both = jnp.where(
-                    lane < LANES // 2, mk[0, i, l, strip, :], mk[chunks - 1, i, l, strip, :]
-                ).astype(jnp.float32)
-                packs[i] = jnp.where(here, pltpu.roll(both, shift, 1), packs[i])
+            for i, (t, source) in enumerate(((0, 0), (chunks - 1, LANES - 1))):
+                m = [mk[t, j, l, strip, :].astype(jnp.float32) for j in range(3)]
+                values = ((0, m[0]), (1, m[0]), (2, m[1]), (3, m[2]))
+                packs[i] = pack([packs[i]], values, r * levels + l, source)[0]
         return tuple(packs)
 
     def middle_strip(strip):
@@ -195,10 +196,12 @@
         for t in range(chunks):
             for l in range(levels):
                 for f in range(8):
-                    to[t, f, l : l + 1, :] = st[t, f, l, row : row + 1, :]
+                    at = f * levels + l
+                    to[t, at : at + 1, :] = st[t, f, l, row : row + 1, :]
                 for f, i in ((8, 2), (9, 0), (10, 1)):
                     mask = mk[t, i, l, row : row + 1, :].astype(jnp.float32)
-                    to[t, f, l : l + 1, :] = mask
+                    at = f * levels + l
+                    to[t, at : at + 1, :] = mask
 
     def remote(src, dst, which, device):
         return pltpu.make_async_remote_copy(
@@ -212,10 +215,10 @@
 
     to_west = remote(own_w, from_e, 0, {"lon": west})
     to_east = remote(own_e, from_w, 1, {"lon": east})
-    to_north = remote(top.at[:, 0:9], from_s, 2, {"lat": lat + 1})
-    to_south = remote(bottom.at[:, 0:8], from_n, 3, {"lat": lat - 1})
+    to_north = remote(top.at[:, 0 : 9 * levels], from_s, 2, {"lat": lat + 1})
+    to_south = remote(bottom.at[:, 0 : 8 * levels], from_n, 3, {"lat": lat - 1})
     to_fold = [
-        remote(top.at[t, 0:8], from_n.at[t], 4 + t, {"lon": partner}) for t in range(chunks)
+        remote(top.at[t, 0 : 8 * levels], from_n.at[t], 4 + t, {"lon": partner}) for t in range(chunks)
     ]
 
     for copy in highest:
@@ -238,11 +241,11 @@
         for copy in to_fold:
             copy.start()
 
-    packs = [nothing] * 9
+    packs = [nothing] * 3
     for l in range(levels):
         x = [st[chunks - 1, f, l, top_strip, :] for f in range(8)]
         x.append(mk[chunks - 1, 1, l, top_strip, :].astype(jnp.float32))
-        packs = pack(packs, x, 2 * ((strips - 1) * levels + l), -1)
+        packs = pack(packs, enumerate(x), (strips - 1) * levels + l, LANES - 1)
     packs = tuple(packs)
     for copy in eastern[0]:
         copy.wait()
@@ -252,7 +255,7 @@
     western = load_tiles(3, 0, 0, high)
     inner = [load_tiles(3 + t, t, 0, high) for t in middle]
     packs = lax.fori_loop(half, strips - 1, eastern_strip, packs)
-    for f in range(9):
+    for f in range(3):
         own_e[f] = packs[f]
 
     @pl.when(has_north)
@@ -267,14 +270,14 @@
     def _():
         to_north.start()
 
-    packs = [nothing] * 8
+    packs = [nothing] * 2
     for l in range(levels):
         x = [st[0, f, l, top_strip, :] for f in range(8)]
-        packs = pack(packs, x, 2 * ((strips - 1) * levels + l), 0)
+        packs = pack(packs, enumerate(x), (strips - 1) * levels + l, 0)
     for copy in western:
         copy.wait()
     packs = lax.fori_loop(0, strips - 1, western_strip, tuple(packs))
-    for f in range(8):
+    for f in range(2):
         own_w[f] = packs[f]
     @pl.when(jnp.logical_and(sends_first, starts))
     def _():
@@ -294,8 +297,8 @@
     def _():
         to_south.start()
 
-    packs = lax.fori_loop(0, strips, outer_flags, (nothing,) * 3)
-    for i in range(3):
+    packs = lax.fori_loop(0, strips, outer_flags, (nothing,) * 2)
+    for i in range(2):
         flags[i] = packs[i]
 
     for t in range(chunks):
@@ -388,12 +391,15 @@
     def _():
         to_west.start()
 
+    def field(ref, t, f):
+        return ref[t, f * levels : (f + 1) * levels, :]
+
     @pl.when(has_south)
     def _():
         to_north.wait_recv()
         for t in range(chunks):
-            h = [from_s[t, f] for f in range(9)]
-            a = [bottom[t, f] for f in range(11)]
+            h = [field(from_s, t, f) for f in range(9)]
+            a = [field(bottom, t, f) for f in range(11)]
             fm = [a[9], a[9], a[10], a[8]]
             speed, mask = advect * h[3], diffuse * h[8]
             for k in range(4):
@@ -412,21 +418,35 @@
 
     to_west.wait_recv()
 
+    def spread(x, g):
+        x = jnp.where(lane // group == g, x, 0.0)
+        x = x + pltpu.roll(x, group, 1)
+        return x + pltpu.roll(x, 2 * group, 1)
+
+    def outer_flux(left, right):
+        speed, mask = spread(left[0], 2), spread(left[2], 0)
+        flux = advect * speed * (left[0] + right[0]) - diffuse * mask * (right[1] - left[1])
+        return flux, mask
+
+    flux_w, _ = outer_flux(from_w, own_w)
+    flux_e, mask = outer_flux(own_e, from_e)
+    rho = haline * pltpu.roll(from_e[0], LANES - group, 1) - thermal * from_e[0]
+    pres = 0.5 * rho
+    level = lane % levels
+    for l in range(1, levels):
+        pres = pres + jnp.where(level >= l, pltpu.roll(rho, l, 1), 0.0)
+    pres = jnp.where(lane // group == 2, pltpu.roll(pres, 2 * group, 1), 0.0)
+    flux_w = flux_w * flags[0]
+    flux_e = -(flux_e + push * mask * pres) * flags[1]
     even = (lane & 1) == 0
-    left = [jnp.where(even, pltpu.roll(from_w[f], 1, 1), own_e[f]) for f in range(9)]
-    right = [jnp.where(even, own_w[f], pltpu.roll(from_e[f], LANES - 1, 1)) for f in range(8)]
-    rho = haline * right[1] - thermal * right[0]
-    pres = 0.5 * rho
-    level = (lane + 1) // 2 % levels
-    for l in range(1, levels):
-        pres = pres + jnp.where(level >= l, pltpu.roll(rho, 2 * l, 1), 0.0)
-    speed, mask = advect * left[2], diffuse * left[8]
-    fm = [flags[0], flags[0], flags[1], flags[2]]
+    pair = ((lane + 1) // 2) & (LANES // 2 - 1)
     for k in range(4):
-        flux = speed * (left[k] + right[k]) - mask * (right[4 + k] - left[4 + k])
-        if k == 2:
-            flux = jnp.where(even, flux, flux + push * left[8] * pres)
-        outer_ref[k] = jnp.where(even, flux, -flux) * fm[k]
+        index = (pair + group * k) & (LANES - 1)
+        one, other = (
+            jnp.take_along_axis(x, index, axis=1, mode="promise_in_bounds")
+            for x in (flux_w, flux_e)
+        )
+        outer_ref[k] = jnp.where(even, one, other)
 
     @pl.when(has_north)
     def _():
@@ -436,21 +456,22 @@
     def _():
         for copy in to_fold:
             copy.wait_recv()
-        mirror = LANES - 1 - lax.broadcasted_iota(jnp.int32, (levels, LANES), 1)
+        shape = from_n.shape[1:]
+        mirror = LANES - 1 - lax.broadcasted_iota(jnp.int32, shape, 1)
+        scalar = lax.broadcasted_iota(jnp.int32, shape, 0) // levels % 4 < 2
 
         def turned(x):
-            return jnp.take_along_axis(x, mirror, axis=1, mode="promise_in_bounds")
+            x = jnp.take_along_axis(x, mirror, axis=1, mode="promise_in_bounds")
+            return jnp.where(scalar, x, -x)
 
         for t in range((chunks + 1) // 2):
-            for f in range(8):
-                sign = 1.0 if f % 4 < 2 else -1.0
-                a, b = from_n[t, f], from_n[chunks - 1 - t, f]
-                from_n[t, f] = sign * turned(b)
-                from_n[chunks - 1 - t, f] = sign * turned(a)
+            a, b = from_n[t], from_n[chunks - 1 - t]
+            from_n[t] = turned(b)
+            from_n[chunks - 1 - t] = turned(a)
 
     for t in range(chunks):
-        h = [top[t, f] for f in range(11)]
-        a = [from_n[t, f] for f in range(8)]
+        h = [field(top, t, f) for f in range(11)]
+        a = [field(from_n, t, f) for f in range(8)]
         fm = [h[9], h[9], h[10], h[8]]
         speed, mask = advect * h[3], diffuse * h[8]
         rho = haline * a[1] - thermal * a[0]
@@ -593,15 +614,15 @@
             pltpu.VMEM((chunks, 4, levels, rows + SUB, LANES), f32),
             pltpu.VMEM((8, levels, SUB, cols), f32),
             pltpu.VMEM((3, levels, SUB, cols), jnp.int32),
-            pltpu.VMEM((9, SUB, LANES), f32),
-            pltpu.VMEM((8, SUB, LANES), f32),
             pltpu.VMEM((3, SUB, LANES), f32),
-            pltpu.VMEM((8, SUB, LANES), f32),
-            pltpu.VMEM((9, SUB, LANES), f32),
-            pltpu.VMEM((chunks, 11, levels, LANES), f32),
-            pltpu.VMEM((chunks, 11, levels, LANES), f32),
-            pltpu.VMEM((chunks, 8, levels, LANES), f32),
-            pltpu.VMEM((chunks, 9, levels, LANES), f32),
+            pltpu.VMEM((2, SUB, LANES), f32),
+            pltpu.VMEM((2, SUB, LANES), f32),
+            pltpu.VMEM((2, SUB, LANES), f32),
+            pltpu.VMEM((3, SUB, LANES), f32),
+            pltpu.VMEM((chunks, 11 * levels, LANES), f32),
+            pltpu.VMEM((chunks, 11 * levels, LANES), f32),
+            pltpu.VMEM((chunks, 8 * levels, LANES), f32),
+            pltpu.VMEM((chunks, 9 * levels, LANES), f32),
             pltpu.SemaphoreType.DMA((chunks + 2, 5)),
             pltpu.SemaphoreType.DMA((4 + chunks,)),
             pltpu.SemaphoreType.DMA((4 + chunks,)),

time: 17.4 us -> 16.6 us (0.954)
  Pallas kernels: 16.6 us -> 15.9 us
    pallas_call x1, Pallas kernels: 14.5 us -> 13.7 us  [shards(): pl.pallas_call(functools.partial(kernel, n_lon, n_lat), out_shape=(out, o...]
where the time goes in v5:
time: 16.6 us; the launch traced here: 16.5 us
  Pallas kernels  15.9 us (96%)
  between operations  0.64 us (4%)
    pallas_call x1, Pallas kernels, shards(): pl.pallas_call(functools.partial(kernel, n_lon, n_lat), out_shape=(out, o...  13.7 us
    pallas_call x1, Pallas kernels, shards(): pl.pallas_call(closing_kernel, out_shape=(out, out), in_specs=[block] * 5...  2.19 us

profile of v5, /device:TPU:26, one launch (start us, length us, event | category | flops | bytes accessed | tf_op | source)
XLA Modules:
  0.0 16.5 jit_solution(2246760693717800906)
XLA Ops:
  0.6 13.7 %shard_map.68 = (f32[4,4,64,512]{3,2,1,0:T(8,128)S(1)}, f32[4,4,64,512]{3,2,1,0:T(8,128)S(1)}, f32[4,8,128]{2,1,0:T(8,128)S(1)}, f32[4,4,4,128]{3,2,1,0:T(4,128)S(1)}, f32[4,4,4,128]{3,2,1,0:T(4,128)S(1)}) custom-call(f32[4,4,64,512]{3,2,1,0:T(8,128)} %bef_hbm.1, f32[4,4,64,512]{3,2,1,0:T(8,128)} %cur_hbm.1, s32[4,64,512]{2,1,0:T(8,128)} %tm_hbm.1, ...), custom_call_target="tpu_custom_call" | custom-call | tf_op jit(solution)/shard_map/pallas_call | solution.py:599
  14.3 2.2 %shard_map.69 = (f32[4,4,64,512]{3,2,1,0:T(8,128)}, f32[4,4,64,512]{3,2,1,0:T(8,128)}) custom-call(f32[4,4,64,512]{3,2,1,0:T(8,128)S(1)} %get-tuple-element.7.after_ref, f32[4,4,64,512]{3,2,1,0:T(8,128)S(1)} %get-tuple-element.8.filt_ref, f32[4,8,128]{2,1,0:T(8,128)S(1)} %get-tuple-element.9.outer_ref, f32[4,4,4,128]{3,2,1,0:T(4,128)S(1)} %get-tuple-element.10.south_ref, ...), custom_call_target="tpu_custom_call" | custom-call | tf_op jit(solution)/shard_map/pallas_call | solution.py:635
